TPU v7x, 256 devices: a whole 4x4x8 slice. The times are simulated.
256 devices in a mesh: bl: 32 (over x, y, core), ch: 8 (over z).
Axes of the slice: x: 4, y: 4, z: 8, core: 2. Of those that a mesh axis runs over, the one named last changes fastest.
Arguments:
- visibilities: float32 [8, 32, 16384], P(None, 'ch', 'bl'), may hold values from -24 to 24
- model: bfloat16 [8, 8, 32, 16384], P(None, None, 'ch', 'bl'), may hold values from -6 to 6
- first_station: int32 [16384], P('bl'), may hold values from 0 to 511
- second_station: int32 [16384], P('bl'), may hold values from 0 to 511
- gain_offset: float32 [8, 8, 32, 512], P(None, None, 'ch', 'bl'), may hold values from -1.5 to 1.5
Outputs:
- smoothed: float32 [8, 8, 32, 512], P(None, None, 'ch', 'bl')
- misfit: float32 [3], replicated
All inputs are finite; a program needn't handle non-finite values.
Results may differ from a plain program's by a relative error of at most 0.0003.
Values sent between devices are 32-bit elements; how exact they have to be, the bound alone decides.
A program may use at most 128 MiB of HBM per device.

v0:
```python
import jax
import jax.numpy as jnp
from jax import lax
from jax.sharding import PartitionSpec as P

STATION_COUNT = 512
ITERS = 3
SPAN = 4


REG = 1.0
KERNEL_VAR = 4.0


def extended(x, sides, width):
    for axis, dim in sides:
        size, length = (lax.axis_size(axis), x.shape[dim])
        up = [(i, (i + 1) % size) for i in range(size - 1)]
        down = [(j, i) for i, j in up]
        last = lax.slice_in_dim(x, length - width, length, axis=dim)
        first = lax.slice_in_dim(x, 0, width, axis=dim)
        before = lax.ppermute(last, axis, up)
        after = lax.ppermute(first, axis, down)
        x = jnp.concatenate([before, x, after], axis=dim)
    return x


def split22(x):
    return [(x[:, 2 * k], x[:, 2 * k + 1]) for k in range(4)]


def join22(m):
    return jnp.stack([m[k][j] for k in range(4) for j in range(2)], axis=1)


def cmul(a, b):
    return (a[0] * b[0] - a[1] * b[1], a[0] * b[1] + a[1] * b[0])


def cadd(a, b):
    return (a[0] + b[0], a[1] + b[1])


def conj(a):
    return (a[0], -a[1])


def matmul22(a, b):
    return [
        cadd(cmul(a[0], b[0]), cmul(a[1], b[2])),
        cadd(cmul(a[0], b[1]), cmul(a[1], b[3])),
        cadd(cmul(a[2], b[0]), cmul(a[3], b[2])),
        cadd(cmul(a[2], b[1]), cmul(a[3], b[3])),
    ]


def herm(a):
    return [conj(a[0]), conj(a[2]), conj(a[1]), conj(a[3])]


def gram_parts(y):
    diag_one = y[0][0] ** 2 + y[0][1] ** 2 + y[1][0] ** 2 + y[1][1] ** 2
    diag_two = y[2][0] ** 2 + y[2][1] ** 2 + y[3][0] ** 2 + y[3][1] ** 2
    off = cadd(cmul(y[0], conj(y[2])), cmul(y[1], conj(y[3])))
    return jnp.stack([diag_one, diag_two, off[0], off[1]], axis=1)


def station_terms(gain_p, gain_q, model, visibilities):
    mod = split22(model.astype(jnp.float32))
    jones_p = split22(gain_p)
    jones_q = split22(gain_q)
    y_one = matmul22(mod, herm(jones_q))
    pred_parts = matmul22(jones_p, y_one)
    y_two = matmul22(herm(mod), herm(jones_p))
    pred = join22(pred_parts)
    resid = visibilities - jnp.sum(pred, axis=0)
    chi = jnp.sum(resid * resid)
    xfull = split22(resid[None] + pred)
    a_one = join22(matmul22(xfull, herm(y_one)))
    a_two = join22(matmul22(herm(xfull), herm(y_two)))
    term_p = jnp.concatenate([a_one, gram_parts(y_one)], axis=1)
    term_q = jnp.concatenate([a_two, gram_parts(y_two)], axis=1)
    return (term_p, term_q, chi)


def accumulate(term_p, term_q, first_station, second_station, count):
    summed = jax.ops.segment_sum(jnp.moveaxis(term_p, 3, 0), first_station, num_segments=count)
    summed = summed + jax.ops.segment_sum(
        jnp.moveaxis(term_q, 3, 0), second_station, num_segments=count
    )
    return jnp.moveaxis(summed, 0, 3)


def solve(normals, gains):
    amat = split22(normals[:, :8])
    diag_one = normals[:, 8] + REG
    diag_two = normals[:, 9] + REG
    off_re = normals[:, 10]
    off_im = normals[:, 11]
    det = diag_one * diag_two - off_re * off_re - off_im * off_im
    zeros = jnp.zeros_like(det)
    inverse = [
        (diag_two / det, zeros),
        (-off_re / det, -off_im / det),
        (-off_re / det, off_im / det),
        (diag_one / det, zeros),
    ]
    fresh = join22(matmul22(amat, inverse))
    return 0.5 * (gains + fresh)


def on_device(visibilities, model, first_station, second_station, gain_offset):
    owned = gain_offset.shape[3]
    chan_dev = gain_offset.shape[2]
    ident = jnp.array([1.0, 0.0, 0.0, 0.0, 0.0, 0.0, 1.0, 0.0], dtype=jnp.float32)
    own_gains = ident[None, :, None, None] + gain_offset
    full = lax.all_gather(own_gains, "bl", axis=3, tiled=True)
    chis = []
    for step in range(ITERS):
        gain_p = jnp.take(full, first_station, axis=3)
        gain_q = jnp.take(full, second_station, axis=3)
        term_p, term_q, chi = station_terms(gain_p, gain_q, model, visibilities)
        chis.append(lax.psum(chi, ("bl", "ch")))
        partial_value = accumulate(term_p, term_q, first_station, second_station, STATION_COUNT)
        normals = lax.psum(partial_value, "bl")
        full = solve(normals, full)
        if step + 1 == ITERS:
            own_gains = lax.dynamic_slice_in_dim(full, lax.axis_index("bl") * owned, owned, 3)
    totals = jnp.stack(chis)
    channel_total = chan_dev * lax.axis_size("ch")
    count_vis = 8.0 * visibilities.shape[2] * lax.axis_size("bl") * channel_total
    misfit = totals / count_vis
    rim = extended(own_gains, (("ch", 2),), SPAN)
    chan = lax.axis_index("ch") * chan_dev + jnp.arange(chan_dev, dtype=jnp.int32)
    numer = jnp.zeros_like(own_gains)
    denom = jnp.zeros((chan_dev,), jnp.float32)
    for shift in range(-SPAN, SPAN + 1):
        weight = jnp.exp(jnp.float32(-(shift * shift) / (2.0 * KERNEL_VAR)))
        numer = numer + weight * rim[:, :, SPAN + shift : SPAN + shift + chan_dev, :]
        valid = ((chan + shift >= 0) & (chan + shift < channel_total)).astype(jnp.float32)
        denom = denom + weight * valid
    smoothed = numer / denom[None, None, :, None]
    return (smoothed, misfit)


def solution(mesh):
    return jax.shard_map(
        on_device,
        mesh=mesh,
        in_specs=(
            P(None, "ch", "bl"),
            P(None, None, "ch", "bl"),
            P("bl"),
            P("bl"),
            P(None, None, "ch", "bl"),
        ),
        out_specs=(P(None, None, "ch", "bl"), P()),
        check_vma=False,
    )
```

profile of v0, /device:TPU:1, one launch (start us, length us, event | category | flops | bytes accessed | tf_op | source)
XLA Modules:
  0.0 1082.0 jit_solution(4368819712197716081)
XLA Ops:
  11.2 36.7 %all_gather.3 = f32[8,8,4,512]{1,0,2,3:T(8,128)S(1)} all-gather(f32[8,8,4,16]{1,0,2,3:T(8,128)S(1)} %copy.1138), channel_id=1, replica_groups=mesh['bl'=32,'ch'=8] {'bl'}, dimensions={3}, use_global_device_ids=true | all-gather | bytes 540672 | tf_op jit(solution)/shard_map/all_gather | solution.py:117
  47.9 4.1 copy.1139
  52.0 1.7 copy-done
  53.7 8.3 gather_fusion
  62.0 5.3 copy.1140
  67.6 8.3 gather_fusion.1
  75.8 5.2 copy.1143
  81.9 1.4 copy.1199
  83.7 3.4 multiply_reduce_fusion.2
  87.0 1.5 copy.1146
  88.6 1.1 broadcast_add_fusion.2
  92.3 8.5 copy.1148
  100.8 4.3 broadcast.331.clone.2
  105.2 67.5 %scatter_fusion.1 = f32[512,8,12,4]{2,1,3,0:T(8,128)} fusion(f32[512,8,12,4]{2,1,3,0:T(8,128)} %broadcast.331.clone.2, s32[512]{0:T(512)S(1)} %copy-done.20, f32[512,8,12,4]{2,1,3,0:T(8,128)} %copy.1148), kind=kCustom, calls=%fused_computation.7 | custom fusion | flops 196608 | bytes 2361344 | tf_op jit(solution)/shard_map/scatter-add | solution.py:88
  172.6 6.1 copy.1150
  181.9 8.5 copy.1147
  190.4 4.3 broadcast.331.clone.1
  194.8 67.4 %scatter_fusion = f32[512,8,12,4]{2,1,3,0:T(8,128)} fusion(f32[512,8,12,4]{2,1,3,0:T(8,128)} %broadcast.331.clone.1, s32[512]{0:T(512)S(1)} %copy-done.21, f32[512,8,12,4]{2,1,3,0:T(8,128)} %copy.1147), kind=kCustom, calls=%fused_computation.6 | custom fusion | flops 196608 | bytes 2361344 | tf_op jit(solution)/shard_map/scatter-add | solution.py:87
  262.1 5.3 copy.1149
  268.6 5.5 copy.1159
  274.1 108.1 %all-reduce.5.cloned.1.call-done = f32[8,12,4,512]{3,0,2,1:T(8,128)} async-done(((f32[8,12,4,512]{3,0,2,1:T(8,128)}), f32[8,12,4,512]{3,0,2,1:T(8,128)}) %all-reduce.5.cloned.1.call-update) | async-done | bytes 786448 | tf_op jit(solution)/shard_map/psum | solution.py:125
  383.3 1.1 subtract_add_fusion.24
  385.7 1.1 subtract_add_fusion.25
  388.2 4.6 copy.1160
  392.8 8.3 gather_fusion.3
  401.1 8.3 gather_fusion.2
  409.4 5.2 copy.1163
  414.6 5.4 copy.1161
  421.7 1.3 copy.1200
  423.0 3.3 multiply_reduce_fusion.1
  426.3 1.5 copy.1166
  427.9 1.1 broadcast_add_fusion.1
  431.7 8.5 copy.1168
  440.3 4.3 broadcast.331.clone.4
  444.6 67.4 %scatter_fusion.3 = f32[512,8,12,4]{2,1,3,0:T(8,128)} fusion(f32[512,8,12,4]{2,1,3,0:T(8,128)} %broadcast.331.clone.4, s32[512]{0:T(512)S(1)} %copy-done.20, f32[512,8,12,4]{2,1,3,0:T(8,128)} %copy.1168), kind=kCustom, calls=%fused_computation.9 | custom fusion | flops 196608 | bytes 2361344 | tf_op jit(solution)/shard_map/scatter-add | solution.py:88
  512.0 6.1 copy.1170
  521.3 8.7 copy.1167
  530.0 4.3 broadcast.331.clone.3
  534.3 67.5 %scatter_fusion.2 = f32[512,8,12,4]{2,1,3,0:T(8,128)} fusion(f32[512,8,12,4]{2,1,3,0:T(8,128)} %broadcast.331.clone.3, s32[512]{0:T(512)S(1)} %copy-done.21, f32[512,8,12,4]{2,1,3,0:T(8,128)} %copy.1167), kind=kCustom, calls=%fused_computation.8 | custom fusion | flops 196608 | bytes 2361344 | tf_op jit(solution)/shard_map/scatter-add | solution.py:87
  601.8 6.1 copy.1169
  607.9 2.2 add_bitcast_fusion.1
  610.2 113.5 %all-reduce.7.cloned.1.call-done = f32[8,12,4,512]{3,0,2,1:T(8,128)} async-done(((f32[8,12,4,512]{3,0,2,1:T(8,128)}), f32[8,12,4,512]{3,0,2,1:T(8,128)}) %all-reduce.7.cloned.1.call-update) | async-done | bytes 786448 | tf_op jit(solution)/shard_map/psum | solution.py:125
  729.7 4.6 copy.1179
  734.3 8.3 gather_fusion.5
  742.6 8.3 gather_fusion.4
  750.9 5.2 copy.1182
  756.1 5.4 copy.1180
  763.2 1.3 copy.1201
  764.5 3.3 multiply_reduce_fusion
  767.9 1.5 copy.1185
  773.2 8.5 copy.1187
  781.7 4.3 broadcast.331.clone.5
  786.0 67.4 %scatter_fusion.5 = f32[512,8,12,4]{2,1,3,0:T(8,128)} fusion(f32[512,8,12,4]{2,1,3,0:T(8,128)} %broadcast.331.clone.5, s32[512]{0:T(512)S(1)} %copy-done.20, f32[512,8,12,4]{2,1,3,0:T(8,128)} %copy.1187), kind=kCustom, calls=%fused_computation.11 | custom fusion | flops 196608 | bytes 2361344 | tf_op jit(solution)/shard_map/scatter-add | solution.py:88
  853.5 5.3 copy.1189
  859.0 7.9 copy.1186
  866.9 4.3 broadcast.331.clone
  871.2 67.4 %scatter_fusion.4 = f32[512,8,12,4]{2,1,3,0:T(8,128)} fusion(f32[512,8,12,4]{2,1,3,0:T(8,128)} %broadcast.331.clone, s32[512]{0:T(512)S(1)} %copy-done.21, f32[512,8,12,4]{2,1,3,0:T(8,128)} %copy.1186), kind=kCustom, calls=%fused_computation.10 | custom fusion | flops 196608 | bytes 2361344 | tf_op jit(solution)/shard_map/scatter-add | solution.py:87
  938.6 5.3 copy.1188
  945.0 77.7 %all-reduce = (f32[1]{0:T(128)}, f32[1]{0:T(128)}, f32[1]{0:T(128)}) all-reduce(f32[1]{0:T(128)} %bitcast.17, f32[1]{0:T(128)} %bitcast.16, f32[1]{0:T(128)} %bitcast.15), channel_id=1, replica_groups=mesh['bl'=32,'ch'=8] {'bl','ch'}, use_global_device_ids=true, to_apply=%region_17.19 | all-reduce | flops 3 | bytes 24 | tf_op jit(solution)/shard_map/psum | solution.py:123
  1022.8 35.8 %all-reduce.9.cloned.1.call-done = f32[8,12,4,512]{3,0,2,1:T(8,128)} async-done(((f32[8,12,4,512]{3,0,2,1:T(8,128)}), f32[8,12,4,512]{3,0,2,1:T(8,128)}) %all-reduce.9.cloned.1.call-update) | async-done | bytes 786448 | tf_op jit(solution)/shard_map/psum | solution.py:125
  1065.6 3.2 collective-permute-start
  1068.7 1.3 collective-permute-start.1
  1070.0 2.5 maximum_multiply_fusion
  1072.5 1.9 collective-permute-done.1
  (201 shorter events, 43.7 us)
Async XLA Ops:
  7.2 375.0 %all-reduce.5.cloned.1.call-start = ((), (), s32[]{:S(2)}) async-start(), calls=%async_computation | async-start | bytes 1572864 | tf_op jit(solution)/shard_map/psum | solution.py:125
  47.9 5.8 copy-start
  53.7 13.7 %copy-start.18 = (bf16[8,8,4,512]{3,2,1,0:T(4,128)(2,1)S(1)}, bf16[8,8,4,512]{3,2,1,0:T(4,128)(2,1)}, u32[]{:S(2)}) copy-start(bf16[8,8,4,512]{3,2,1,0:T(4,128)(2,1)} %param.9) | copy-start | bytes 786436
  75.8 7.4 copy-start.19
  81.7 5.3 copy-start.6
  90.6 0.9 copy-start.11
  91.4 0.9 copy-start.15
  92.3 12.8 %copy-start.20 = (s32[512]{0:T(512)S(1)}, s32[512]{0:T(512)}, u32[]{:S(2)}) copy-start(s32[512]{0:T(512)} %param.11) | copy-start | bytes 6148
  181.9 12.8 %copy-start.21 = (s32[512]{0:T(512)S(1)}, s32[512]{0:T(512)}, u32[]{:S(2)}) copy-start(s32[512]{0:T(512)} %param.10) | copy-start | bytes 6148
  190.4 77.0 %copy-start.3 = (f32[512,8,12,4]{0,1,3,2:T(8,128)S(1)}, f32[512,8,12,4]{0,1,3,2:T(8,128)}, u32[]{:S(2)}) copy-start(f32[512,8,12,4]{0,1,3,2:T(8,128)} %copy.1150) | copy-start | bytes 2359300
  268.5 455.1 %all-reduce.7.cloned.1.call-start = ((), (), s32[]{:S(2)}) async-start(), calls=%async_computation.1 | async-start | bytes 1572864 | tf_op jit(solution)/shard_map/psum | solution.py:125
  388.2 26.4 %copy-start.1 = (f32[8,8,4,512]{3,1,2,0:T(8,128)}, f32[8,8,4,512]{3,1,2,0:T(8,128)S(1)}, u32[]{:S(2)}) copy-start(f32[8,8,4,512]{3,1,2,0:T(8,128)S(1)} %add_multiply_fusion.1) | copy-start | bytes 1572868
  414.6 5.6 copy-start.10
  421.5 4.8 copy-start.7
  429.9 0.9 copy-start.12
  430.8 1.0 copy-start.16
  530.0 77.9 %copy-start.4 = (f32[512,8,12,4]{0,1,3,2:T(8,128)S(1)}, f32[512,8,12,4]{0,1,3,2:T(8,128)}, u32[]{:S(2)}) copy-start(f32[512,8,12,4]{0,1,3,2:T(8,128)} %copy.1170) | copy-start | bytes 2359300
  601.8 127.8 %copy-start.2 = (f32[8,8,4,512]{3,1,2,0:T(8,128)S(1)}, f32[8,8,4,512]{3,1,2,0:T(8,128)}, u32[]{:S(2)}) copy-start(f32[8,8,4,512]{3,1,2,0:T(8,128)} %copy-done.1) | copy-start | bytes 1572868
  610.1 448.5 %all-reduce.9.cloned.1.call-start = ((), (), s32[]{:S(2)}) async-start(), calls=%async_computation.2 | async-start | bytes 1572864 | tf_op jit(solution)/shard_map/psum | solution.py:125
  729.7 26.4 %copy-start.5 = (f32[8,8,4,512]{3,1,2,0:T(8,128)}, f32[8,8,4,512]{3,1,2,0:T(8,128)S(1)}, u32[]{:S(2)}) copy-start(f32[8,8,4,512]{3,1,2,0:T(8,128)S(1)} %add_multiply_fusion) | copy-start | bytes 1572868
  756.1 5.6 copy-start.9
  763.0 4.8 copy-start.8
  771.4 0.9 copy-start.13
  772.2 1.0 copy-start.17
  781.7 77.0 %copy-start.14 = (f32[8,12,4,512]{3,0,2,1:T(8,128)S(1)}, f32[8,12,4,512]{3,0,2,1:T(8,128)}, u32[]{:S(2)}) copy-start(f32[8,12,4,512]{3,0,2,1:T(8,128)} %copy-done.13) | copy-start | bytes 2359300
  1065.6 7.0 collective-permute-start
  1068.7 5.7 collective-permute-start.1
Sparse Core Ops, SparseCore 0:
  268.6 113.4 all-reduce.4
  610.2 113.3 all-reduce.6
  945.1 113.4 all-reduce.8
where the time goes:
time: 1090 us; the launch traced here: 1080 us
  other arithmetic  457 us (42%)
  waiting for transfers between devices  259 us (24%)
  local copies, waits for them, and re-layouts  232 us (21%)
  blocking collectives  114 us (10%)
  between operations  15.1 us (1%)
    psum x3, waiting for transfers between devices, on_device(): normals = lax.psum(partial_value, 'bl')  257 us
    scatter-add x3, other arithmetic, accumulate(): jax.ops.segment_sum(jnp.moveaxis(term_q, 3, 0), second_station, num_segme...  202 us
    scatter-add x3, other arithmetic, accumulate(): jax.ops.segment_sum(jnp.moveaxis(term_p, 3, 0), first_station, num_segmen...  202 us
    psum x1, blocking collectives, on_device(): chis.append(lax.psum(chi, ('bl', 'ch')))  77.7 us
    gather x6, local copies, waits for them, and re-layouts, on_device(): gain_p = jnp.take(full, first_station, axis=3)  41 us
    gather x6, local copies, waits for them, and re-layouts, on_device(): gain_q = jnp.take(full, second_station, axis=3)  40.5 us
    all_gather x1, blocking collectives, on_device(): full = lax.all_gather(own_gains, 'bl', axis=3, tiled=True)  36.7 us
    another operation x6, local copies, waits for them, and re-layouts  25.8 us
  transfers between devices with their start and end apart: 5, of which 4 were waited for; matrix products, arithmetic and copies ran while one was open for 1% of the time, Pallas kernels for 0%

commit v1 on v0

v1 whole, which is shorter than its diff:
```python
import functools

import jax
import jax.numpy as jnp
from jax import lax
from jax.experimental import pallas as pl
from jax.experimental.pallas import tpu as pltpu
from jax.sharding import PartitionSpec as P

STATION_COUNT = 512
ITERS = 3
SPAN = 4
REG = 1.0
KERNEL_VAR = 4.0
BLOCK = 256
F32 = jnp.float32
BF16 = jnp.bfloat16


def cmul(a, b):
    return (a[0] * b[0] - a[1] * b[1], a[0] * b[1] + a[1] * b[0])


def cadd(a, b):
    return (a[0] + b[0], a[1] + b[1])


def conj(a):
    return (a[0], -a[1])


def matmul22(a, b):
    return [
        cadd(cmul(a[0], b[0]), cmul(a[1], b[2])),
        cadd(cmul(a[0], b[1]), cmul(a[1], b[3])),
        cadd(cmul(a[2], b[0]), cmul(a[3], b[2])),
        cadd(cmul(a[2], b[1]), cmul(a[3], b[3])),
    ]


def herm(a):
    return [conj(a[0]), conj(a[2]), conj(a[1]), conj(a[3])]


def gram_parts(y):
    diag_one = y[0][0] ** 2 + y[0][1] ** 2 + y[1][0] ** 2 + y[1][1] ** 2
    diag_two = y[2][0] ** 2 + y[2][1] ** 2 + y[3][0] ** 2 + y[3][1] ** 2
    off = cadd(cmul(y[0], conj(y[2])), cmul(y[1], conj(y[3])))
    return [diag_one, diag_two, off[0], off[1]]


def flat(m):
    return [m[k][j] for k in range(4) for j in range(2)]


def pairs(parts):
    return [(parts[2 * k], parts[2 * k + 1]) for k in range(4)]


def nt_dot(a, b):
    return lax.dot_general(a, b, (((1,), (1,)), ((), ())), preferred_element_type=F32)


def kernel(
    chips,
    nch,
    model_ref,
    vis_ref,
    stat_ref,
    goff_ref,
    out_ref,
    chi_ref,
    m_all,
    m_stage,
    v_all,
    s_all,
    onehot,
    gains,
    gains_hl,
    own_t,
    term_a,
    term_b,
    norm,
    recv,
    chi_acc,
    fin,
    chi_send,
    chi_recv,
    ex_send,
    ex_recv,
    rs_send,
    rs_recv,
    ag_send,
    ag_recv,
    fin_send,
    fin_recv,
    chi_ssem,
    chi_rsem,
):
    nb = vis_ref.shape[2]
    total_b = 2 * nb
    st = STATION_COUNT // chips
    half = st // 2
    rows = st + half
    me = lax.axis_index("bl")
    z = lax.axis_index("ch")
    chip = me // 2
    core = me % 2
    sib = chip * 2 + (1 - core)

    def there(bl, ch=None):
        return {"bl": bl, "ch": z if ch is None else ch}

    def peer(k):
        return (chip + k) % chips

    def send(src, dst, ssem, rsem, where):
        return pltpu.make_async_remote_copy(
            src_ref=src, dst_ref=dst, send_sem=ssem, recv_sem=rsem,
            device_id=where, device_id_type=pl.DeviceIdType.MESH)

    barrier = pltpu.get_barrier_semaphore()

    def greet_bl(k, carry):
        pl.semaphore_signal(barrier, inc=1, device_id=there(peer(k) * 2 + core),
                            device_id_type=pl.DeviceIdType.MESH)
        return carry

    def greet_ch(k, carry):
        pl.semaphore_signal(
            barrier, inc=1,
            device_id=there(chip * 2 + (core + k) % 2, (z + k // 2) % nch),
            device_id_type=pl.DeviceIdType.MESH)
        return carry

    lax.fori_loop(1, 2 * nch, greet_ch, 0)
    lax.fori_loop(1, chips, greet_bl, 0)

    r = lax.broadcasted_iota(jnp.int32, (256, 256), 0)
    q = lax.broadcasted_iota(jnp.int32, (256, 256), 1)
    h = lax.shift_right_logical(r, 7)
    c_two = lax.shift_right_logical(r, 6) & 1
    comp = lax.shift_right_logical(r, 3) & 7
    direction = r & 7
    chan = 2 * ((core + h) & 1) + c_two
    perm = jnp.where(q == direction * 32 + comp * 4 + chan, 1.0, 0.0).astype(BF16)
    permuted = jnp.dot(perm, model_ref[...], preferred_element_type=F32)
    m_all[:, :nb] = permuted[:128]
    m_stage[...] = permuted[128:]
    v_all[:, :nb] = vis_ref[0]
    s_all[:, :nb] = stat_ref[...]
    own_rows = pl.ds(pl.multiple_of(me * half, half), half)
    gains[own_rows, :] = goff_ref[0]

    pl.semaphore_wait(barrier, 2 * nch - 1 + chips - 1)

    swaps = [
        send(goff_ref.at[1], gains.at[own_rows, :], ex_send.at[0], ex_recv.at[0], there(sib)),
        send(stat_ref, s_all.at[:, pl.ds(nb, nb)], ex_send.at[1], ex_recv.at[1], there(sib)),
        send(m_stage, m_all.at[:, pl.ds(nb, nb)], ex_send.at[2], ex_recv.at[2], there(sib)),
        send(vis_ref.at[1], v_all.at[:, pl.ds(nb, nb)], ex_send.at[3], ex_recv.at[3], there(sib)),
    ]
    for swap in swaps:
        swap.start()
    chip_rows = pl.ds(pl.multiple_of(chip * st, st), st)

    def ag_copy(k):
        return send(gains.at[chip_rows, :], gains.at[chip_rows, :],
                    ag_send.at[k - 1], ag_recv.at[k - 1], there(peer(k) * 2 + core))

    def ag_start(k, carry):
        ag_copy(k).start()
        return carry

    def ag_wait_recv(k, carry):
        ag_copy(k).wait_recv()
        return carry

    def ag_wait_send(k, carry):
        ag_copy(k).wait_send()
        return carry

    swaps[0].wait_recv()
    lax.fori_loop(1, chips, ag_start, 0)
    own_t[...] = jnp.transpose(gains[chip_rows, :])

    station = lax.broadcasted_iota(jnp.int32, (STATION_COUNT, BLOCK), 0)

    def hot(i, carry):
        at = pl.multiple_of(i * BLOCK, BLOCK)
        for j in range(2):
            which = s_all[j:j + 1, pl.ds(at, BLOCK)]
            onehot[:, pl.ds(pl.multiple_of(j * total_b + at, BLOCK), BLOCK)] = jnp.where(
                station == which, 1.0, 0.0).astype(BF16)
        return carry

    lax.fori_loop(0, nb // BLOCK, hot, 0)
    swaps[1].wait_recv()
    lax.fori_loop(nb // BLOCK, total_b // BLOCK, hot, 0)
    swaps[2].wait_recv()
    swaps[3].wait_recv()
    for swap in swaps:
        swap.wait_send()
    chi_acc[...] = jnp.zeros_like(chi_acc)
    lax.fori_loop(1, chips, ag_wait_recv, 0)
    lax.fori_loop(1, chips, ag_wait_send, 0)

    def store_pair(ref, at_row, lo_row, cols, one, two, dup):
        both = jnp.concatenate([one, two], axis=0)
        hi = both.astype(BF16)
        lo = (both - hi.astype(F32)).astype(BF16)
        ref[at_row:at_row + 16, cols] = hi
        ref[lo_row:lo_row + 16, cols] = lo
        if dup:
            ref[at_row + dup:at_row + dup + 16, cols] = hi
            ref[lo_row + dup:lo_row + dup + 16, cols] = lo

    def terms(step):
        def body(i, carry):
            at = pl.multiple_of(i * BLOCK, BLOCK)
            cols = pl.ds(at, BLOCK)
            cols_q = pl.ds(pl.multiple_of(total_b + at, BLOCK), BLOCK)
            both = gains_hl[...]
            gp = jnp.dot(both, onehot[:, cols], preferred_element_type=F32)
            gp = gp[:128] + gp[128:]
            gq = jnp.dot(both, onehot[:, cols_q], preferred_element_type=F32)
            gq = gq[:128] + gq[128:]
            chi = jnp.zeros((1, BLOCK), F32)
            for c in range(2):
                def part(x):
                    return pairs([x[c * 64 + 8 * k:c * 64 + 8 * k + 8] for k in range(8)])

                jp = part(gp)
                jq = part(gq)
                mod = pairs([m_all[c * 64 + 8 * k:c * 64 + 8 * k + 8, cols] for k in range(8)])
                y_one = matmul22(mod, herm(jq))
                pred = flat(matmul22(jp, y_one))
                y_two = matmul22(herm(mod), herm(jp))
                resid = []
                for k in range(8):
                    one = v_all[c * 8 + k:c * 8 + k + 1, cols] - jnp.sum(pred[k], axis=0, keepdims=True)
                    chi = chi + one * one
                    resid.append(one)
                resid = pairs(resid)
                a_one = flat(matmul22(resid, herm(y_one)))
                a_two = flat(matmul22(herm(resid), herm(y_two)))
                b_one = gram_parts(y_one)
                b_two = gram_parts(y_two)
                for k in range(0, 8, 2):
                    row = c * 64 + 8 * k
                    store_pair(term_a, row, 128 + row, cols, a_one[k], a_one[k + 1], 0)
                    store_pair(term_a, row, 128 + row, cols_q, a_two[k], a_two[k + 1], 0)
                for k in range(0, 4, 2):
                    row = c * 32 + 8 * k
                    store_pair(term_b, row, 128 + row, cols, b_one[k], b_one[k + 1], 64)
                    store_pair(term_b, row, 128 + row, cols_q, b_two[k], b_two[k + 1], 64)
            sums = chi[:, :128]
            for j in range(128, BLOCK, 128):
                sums = sums + chi[:, j:j + 128]
            chi_acc[pl.ds(step, 1), :] += sums
            return carry

        lax.fori_loop(0, total_b // BLOCK, body, 0)

    lane = lax.broadcasted_iota(jnp.int32, (half, 128), 1)

    def iteration(step, last):
        size = rows + 8 if last else rows
        turned = jnp.transpose(gains[...])
        hi = turned.astype(BF16)
        gains_hl[:128] = hi
        gains_hl[128:] = (turned - hi.astype(F32)).astype(BF16)
        terms(step)
        group = max(st, 256)

        for g in range(STATION_COUNT // group):
            hot_rows = onehot[g * group:(g + 1) * group, :]
            na = nt_dot(hot_rows, term_a[...])
            na = na[:, :128] + na[:, 128:]
            nb_ = nt_dot(hot_rows, term_b[...])
            nb_ = nb_[:, :128] + nb_[:, 128:]
            for j in range(group // st):
                chunk = g * (group // st) + j
                norm[chunk, :st, :] = na[j * st:(j + 1) * st]
                norm[chunk, st:rows, :] = jnp.where(
                    lane < 64, nb_[j * st:j * st + half], nb_[j * st + half:(j + 1) * st])
                if last:
                    norm[chunk, rows:rows + 8, :] = chi_acc[...]

        def rs_copy(k):
            return send(norm.at[peer(k), pl.ds(0, size), :],
                        recv.at[k - 1, pl.ds(0, size), :],
                        rs_send.at[k - 1], rs_recv.at[k - 1], there(peer(k) * 2 + core))

        def rs_start(k, carry):
            rs_copy(k).start()
            return carry

        lax.fori_loop(1, chips, rs_start, 0)

        def rs_take(k, total):
            rs_copy(k).wait_recv()
            return total + recv[k - 1, :size, :]

        total = lax.fori_loop(1, chips, rs_take, norm[chip, :size, :])

        def rs_wait_send(k, carry):
            rs_copy(k).wait_send()
            return carry

        r_t = jnp.transpose(total[:st])
        packed = total[st:rows]
        unpacked = jnp.concatenate([packed, pltpu.roll(packed, 64, 1)], axis=0)
        b_t = jnp.transpose(unpacked)
        fresh_rows = []
        for c in range(2):
            old = [own_t[c * 64 + 8 * k:c * 64 + 8 * k + 8, :] for k in range(8)]
            amat = pairs([r_t[c * 64 + 8 * k:c * 64 + 8 * k + 8, :] - old[k] for k in range(8)])
            diag_one, diag_two, off_re, off_im = [
                b_t[c * 32 + 8 * k:c * 32 + 8 * k + 8, :] for k in range(4)]
            diag_one = diag_one + REG
            diag_two = diag_two + REG
            det = diag_one * diag_two - off_re * off_re - off_im * off_im
            scale = 0.5 / det
            d_one = diag_one * scale
            d_two = diag_two * scale
            o_re = off_re * scale
            o_im = off_im * scale
            for row in range(2):
                a0 = amat[2 * row]
                a1 = amat[2 * row + 1]
                n0 = cadd((a0[0] * d_two, a0[1] * d_two), cmul(a1, (-o_re, o_im)))
                n1 = cadd(cmul(a0, (-o_re, -o_im)), (a1[0] * d_one, a1[1] * d_one))
                k = 4 * row
                fresh_rows += [old[k] + n0[0], old[k + 1] + n0[1],
                               old[k + 2] + n1[0], old[k + 3] + n1[1]]
        fresh = jnp.concatenate(fresh_rows, axis=0)
        own_t[...] = fresh
        gains[chip_rows, :] = jnp.transpose(fresh)
        if not last:
            lax.fori_loop(1, chips, ag_start, 0)
        lax.fori_loop(1, chips, rs_wait_send, 0)
        if not last:
            lax.fori_loop(1, chips, ag_wait_recv, 0)
            lax.fori_loop(1, chips, ag_wait_send, 0)
        return total[rows:] if last else None

    def early(step, carry):
        iteration(step, False)
        return carry

    lax.fori_loop(0, ITERS - 1, early, 0)
    chi_total = iteration(ITERS - 1, True)

    chi_send[...] = chi_total
    base = chip * st

    def half_rows(which):
        return pl.ds(pl.multiple_of(base + which * half, half), half)

    def chi_copy(k):
        return send(chi_send, chi_recv.at[k - 1], chi_ssem.at[k - 1], chi_rsem.at[k - 1],
                    there(chip * 2 + (core + k) % 2, (z + k // 2) % nch))

    def up(which):
        return send(gains.at[half_rows(which), :], fin.at[0, core], fin_send.at[which],
                    fin_recv.at[0, core], there(chip * 2 + which, (z + 1) % nch))

    def down(which):
        return send(gains.at[half_rows(which), :], fin.at[2, core], fin_send.at[2 + which],
                    fin_recv.at[2, core], there(chip * 2 + which, (z + nch - 1) % nch))

    across = send(gains.at[half_rows(1 - core), :], fin.at[1, core], fin_send.at[4],
                  fin_recv.at[1, core], there(sib))

    across.start()

    @pl.when(z < nch - 1)
    def _():
        for which in range(2):
            up(which).start()

    @pl.when(z > 0)
    def _():
        for which in range(2):
            down(which).start()

    def chi_start(k, carry):
        chi_copy(k).start()
        return carry

    lax.fori_loop(1, 2 * nch, chi_start, 0)
    fin[1, core] = gains[half_rows(core), :]

    def wait_fin(slot, source):
        send(fin.at[slot, source], fin.at[slot, source], fin_send.at[0],
             fin_recv.at[slot, source], there(sib)).wait_recv()

    @pl.when(z > 0)
    def _():
        for source in range(2):
            wait_fin(0, source)

    @pl.when(z == 0)
    def _():
        fin[0] = jnp.zeros(fin.shape[1:], F32)

    @pl.when(z < nch - 1)
    def _():
        for source in range(2):
            wait_fin(2, source)

    @pl.when(z == nch - 1)
    def _():
        fin[2] = jnp.zeros(fin.shape[1:], F32)

    wait_fin(1, 1 - core)

    slabs = []
    for slot in range(3):
        for source in range(2):
            turned = jnp.transpose(fin[slot, source])
            slabs += [turned[:64], turned[64:]]
    weights = [jnp.exp(jnp.full((1, 1), -(s * s) / (2.0 * KERNEL_VAR), F32)) for s in range(-SPAN, SPAN + 1)]
    for c in range(4):
        numer = jnp.zeros_like(slabs[0])
        denom = jnp.zeros((1, 1), F32)
        for s in range(-SPAN, SPAN + 1):
            weight = weights[s + SPAN]
            numer = numer + weight * slabs[4 + c + s]
            at = z * 4 + c + s
            valid = jnp.where((at >= 0) & (at < 4 * nch), 1.0, 0.0).astype(F32)
            denom = denom + weight * valid
        out_ref[c] = numer / denom

    def chi_take(k, total):
        chi_copy(k).wait_recv()
        return total + chi_recv[k - 1]

    chi_all = lax.fori_loop(1, 2 * nch, chi_take, chi_total)
    chi_ref[...] = jnp.broadcast_to(jnp.sum(chi_all, axis=1, keepdims=True), (8, 128))

    def chi_wait_send(k, carry):
        chi_copy(k).wait_send()
        return carry

    lax.fori_loop(1, 2 * nch, chi_wait_send, 0)
    across.wait_send()

    @pl.when(z < nch - 1)
    def _():
        for which in range(2):
            up(which).wait_send()

    @pl.when(z > 0)
    def _():
        for which in range(2):
            down(which).wait_send()


def on_device(visibilities, model, first_station, second_station, gain_offset):
    nb = visibilities.shape[2]
    half = gain_offset.shape[3]
    st = 2 * half
    chips = lax.axis_size("bl") // 2
    nch = lax.axis_size("ch")
    rows = st + half
    total_b = 2 * nb
    core = lax.axis_index("bl") % 2
    mine = core == 0

    model2d = model.reshape(256, nb)
    vis = jnp.transpose(visibilities, (1, 0, 2)).reshape(2, 16, nb)
    vis = jnp.where(mine, vis, vis[::-1])
    stat = jnp.concatenate([first_station[None], second_station[None], jnp.zeros((6, nb), jnp.int32)], axis=0)
    ident = jnp.array([1.0, 0.0, 0.0, 0.0, 0.0, 0.0, 1.0, 0.0], dtype=F32)
    goff = ident[None, :, None, None] + gain_offset
    goff = jnp.transpose(goff, (2, 3, 1, 0)).reshape(2, 2, half, 64)
    goff = jnp.transpose(goff, (0, 2, 1, 3)).reshape(2, half, 128)
    goff = jnp.where(mine, goff, goff[::-1])

    vmem = pl.BlockSpec(memory_space=pltpu.VMEM)
    dma = pltpu.SemaphoreType.DMA
    smooth, chi = pl.pallas_call(
        functools.partial(kernel, chips, nch),
        out_shape=(
            jax.ShapeDtypeStruct((4, 64, half), F32),
            jax.ShapeDtypeStruct((8, 128), F32),
        ),
        in_specs=[vmem] * 4,
        out_specs=(vmem, vmem),
        scratch_shapes=[
            pltpu.VMEM((128, total_b), F32),
            pltpu.VMEM((128, nb), F32),
            pltpu.VMEM((16, total_b), F32),
            pltpu.VMEM((8, total_b), jnp.int32),
            pltpu.VMEM((STATION_COUNT, 2 * total_b), BF16),
            pltpu.VMEM((STATION_COUNT, 128), F32),
            pltpu.VMEM((256, STATION_COUNT), BF16),
            pltpu.VMEM((128, st), F32),
            pltpu.VMEM((256, 2 * total_b), BF16),
            pltpu.VMEM((256, 2 * total_b), BF16),
            pltpu.VMEM((chips, rows + 8, 128), F32),
            pltpu.VMEM((chips - 1, rows + 8, 128), F32),
            pltpu.VMEM((8, 128), F32),
            pltpu.VMEM((3, 2, half, 128), F32),
            pltpu.VMEM((8, 128), F32),
            pltpu.VMEM((2 * nch - 1, 8, 128), F32),
            dma((4,)),
            dma((4,)),
            dma((chips - 1,)),
            dma((chips - 1,)),
            dma((chips - 1,)),
            dma((chips - 1,)),
            dma((5,)),
            dma((3, 2)),
            dma((2 * nch - 1,)),
            dma((2 * nch - 1,)),
        ],
        compiler_params=pltpu.CompilerParams(
            collective_id=0, has_side_effects=True, vmem_limit_bytes=48 * 1024 * 1024),
    )(model2d, vis, stat, goff)
    smoothed = jnp.transpose(smooth.reshape(4, 8, 8, half), (2, 1, 0, 3))
    count_vis = 8.0 * nb * lax.axis_size("bl") * 4 * nch
    misfit = chi[:ITERS, 0] / count_vis
    return (smoothed, misfit)


def solution(mesh):
    return jax.shard_map(
        on_device,
        mesh=mesh,
        in_specs=(
            P(None, "ch", "bl"),
            P(None, None, "ch", "bl"),
            P("bl"),
            P("bl"),
            P(None, None, "ch", "bl"),
        ),
        out_specs=(P(None, None, "ch", "bl"), P()),
        check_vma=False,
    )
```

time: 1090 us -> 75.2 us (0.07)
  other arithmetic: 457 us -> 0.8 us
  waiting for transfers between devices: 259 us -> 0 us
  local copies, waits for them, and re-layouts: 232 us -> 3.95 us
  blocking collectives: 114 us -> 0 us
  Pallas kernels: 0 us -> 69.5 us
  between operations: 15.1 us -> 0.72 us
    scatter-add x6 -> x0, other arithmetic: 405 us -> none  [the longest x3 202 us: accumulate(): jax.ops.segment_sum(jnp.moveaxis(term_q, 3, 0), second_station, num_segme...]
    psum x3 -> x0, waiting for transfers between devices: 257 us -> none  [on_device(): normals = lax.psum(partial_value, 'bl')]
    gather x12 -> x0, local copies, waits for them, and re-layouts: 81.5 us -> none  [the longest x6 41 us: on_device(): gain_p = jnp.take(full, first_station, axis=3)]
    psum x1 -> x0, blocking collectives: 77.7 us -> none  [on_device(): chis.append(lax.psum(chi, ('bl', 'ch')))]
    pallas_call x0 -> x1, Pallas kernels: none -> 69.5 us  [on_device(): pl.pallas_call(functools.partial(kernel, chips, nch), out_shape=(jax.Shap...]
    transpose x6 -> x2, local copies, waits for them, and re-layouts: 50.6 us -> 0.98 us  [the longest x1 0.9 us: on_device(): vis = jnp.transpose(visibilities, (1, 0, 2)).reshape(2, 16, nb)]
    all_gather x1 -> x0, blocking collectives: 36.7 us -> none  [on_device(): full = lax.all_gather(own_gains, 'bl', axis=3, tiled=True)]
    scatter-add x6 -> x0, local copies, waits for them, and re-layouts: 34.1 us -> none  [the longest x3 17.4 us: accumulate(): jax.ops.segment_sum(jnp.moveaxis(term_q, 3, 0), second_station, num_segme...]
  transfers between devices with their start and end apart: 5 -> 0, of which waited for: 4 -> 0; matrix products, arithmetic and copies ran while one was open for 1% -> 0% of each run, Pallas kernels for 0% -> 0%
where the time goes in v1:
time: 75.2 us; the launch traced here: 75 us
  Pallas kernels  69.5 us (92%)
  local copies, waits for them, and re-layouts  3.95 us (5%)
  other arithmetic  0.8 us (1%)
    pallas_call x1, Pallas kernels, on_device(): pl.pallas_call(functools.partial(kernel, chips, nch), out_shape=(jax.Shap...  69.5 us
    unnamed x10, local copies, waits for them, and re-layouts  2.02 us

profile of v1, /device:TPU:1, one launch (start us, length us, event | category | flops | bytes accessed | tf_op | source)
XLA Modules:
  0.0 75.0 jit_solution(17125721253866374727)
XLA Ops:
  0.6 0.0 copy-start.3
  0.7 0.0 copy-start.2
  0.7 0.1 pad.2.clone
  0.7 0.6 copy-done.3
  1.3 0.0 copy-done.2
  1.3 0.1 add_add_fusion.stat_ref
  1.4 0.0 copy-start.1
  1.4 0.9 %copy.10 = f32[4,8,512]{2,1,0:T(8,128)S(1)} copy(f32[4,8,512]{2,0,1:T(4,128)} %bitcast.19) | data formatting | bytes 131072 | tf_op jit(solution)/shard_map/transpose | solution.py:473
  2.3 0.0 copy-start.4
  2.3 0.0 copy-done.1
  2.4 0.6 copy-done.4
  3.0 0.1 add_bitcast_fusion
  3.1 0.0 copy-start
  3.1 0.1 copy.11
  3.2 0.1 copy.14
  3.2 0.8 %copy-done = bf16[8,8,4,512]{3,2,1,0:T(4,128)(2,1)S(1)} copy-done((bf16[8,8,4,512]{3,2,1,0:T(4,128)(2,1)S(1)}, bf16[8,8,4,512]{3,2,1,0:T(4,128)(2,1)}, u32[]{:S(2)}) %copy-start) | copy-done | bytes 262168
  4.0 0.1 reshape.22.model_ref
  4.1 69.5 %shard_map.77 = (f32[4,64,16]{2,1,0:T(8,128)S(1)}, f32[8,128]{1,0:T(8,128)S(1)}) custom-call(bf16[256,512]{1,0:T(8,128)(2,1)S(1)} %reshape.22.model_ref, f32[2,16,512]{2,1,0:T(8,128)S(1)} %reverse_select_fusion.vis_ref, s32[8,512]{1,0:T(8,128)S(1)} %add_add_fusion.stat_ref, f32[2,16,128]{2,1,0:T(8,128)S(1)} %reverse_select_fusion.1.goff_ref), custom_call_target="tpu_custom_call" | custom-call | tf_op jit(solution)/shard_map/pallas_call | solution.py:484
  73.6 0.7 copy.16
  74.4 0.6 multiply_reduce_fusion
  (3 shorter events, 0.0 us)
Async XLA Ops:
  0.6 0.7 copy-start.3
  0.7 0.7 copy-start.2
  1.4 0.9 %copy-start.1 = (f32[8,8,4,16]{3,2,1,0:T(4,128)S(1)}, f32[8,8,4,16]{3,2,1,0:T(4,128)}, u32[]{:S(2)}) copy-start(f32[8,8,4,16]{3,2,1,0:T(4,128)} %param.10) | copy-start | bytes 49156
  2.3 0.7 copy-start.4
  3.1 1.0 %copy-start = (bf16[8,8,4,512]{3,2,1,0:T(4,128)(2,1)S(1)}, bf16[8,8,4,512]{3,2,1,0:T(4,128)(2,1)}, u32[]{:S(2)}) copy-start(bf16[8,8,4,512]{3,2,1,0:T(4,128)(2,1)} %param.7) | copy-start | bytes 786436

commit v2 on v0

v2 whole, which is shorter than its diff:
```python
import functools

import jax
import jax.numpy as jnp
from jax import lax
from jax.experimental import pallas as pl
from jax.experimental.pallas import tpu as pltpu
from jax.sharding import PartitionSpec as P

STATION_COUNT = 512
ITERS = 3
SPAN = 4
REG = 1.0
KERNEL_VAR = 4.0
BLOCK = 256
F32 = jnp.float32
BF16 = jnp.bfloat16


def cmul(a, b):
    return (a[0] * b[0] - a[1] * b[1], a[0] * b[1] + a[1] * b[0])


def cadd(a, b):
    return (a[0] + b[0], a[1] + b[1])


def conj(a):
    return (a[0], -a[1])


def matmul22(a, b):
    return [
        cadd(cmul(a[0], b[0]), cmul(a[1], b[2])),
        cadd(cmul(a[0], b[1]), cmul(a[1], b[3])),
        cadd(cmul(a[2], b[0]), cmul(a[3], b[2])),
        cadd(cmul(a[2], b[1]), cmul(a[3], b[3])),
    ]


def herm(a):
    return [conj(a[0]), conj(a[2]), conj(a[1]), conj(a[3])]


def gram_parts(y):
    diag_one = y[0][0] ** 2 + y[0][1] ** 2 + y[1][0] ** 2 + y[1][1] ** 2
    diag_two = y[2][0] ** 2 + y[2][1] ** 2 + y[3][0] ** 2 + y[3][1] ** 2
    off = cadd(cmul(y[0], conj(y[2])), cmul(y[1], conj(y[3])))
    return [diag_one, diag_two, off[0], off[1]]


def flat(m):
    return [m[k][j] for k in range(4) for j in range(2)]


def pairs(parts):
    return [(parts[2 * k], parts[2 * k + 1]) for k in range(4)]


def nt_dot(a, b):
    return lax.dot_general(a, b, (((1,), (1,)), ((), ())), preferred_element_type=F32)


def plane(chips):
    ny = 1
    while ny * ny < chips:
        ny *= 2
    return (chips // ny, ny)


def far_first(chips):
    nx, ny = plane(chips)

    def hops(o):
        return min(o[0], nx - o[0]) + min(o[1], ny - o[1])

    others = [(i, j) for i in range(nx) for j in range(ny) if i + j > 0]
    return sorted(others, key=lambda o: -hops(o))


def kernel(
    chips,
    nch,
    vis_hbm,
    model_hbm,
    first_hbm,
    second_hbm,
    goff_hbm,
    out_ref,
    chi_ref,
    vis_in,
    model_in,
    first_in,
    second_in,
    goff_in,
    m_all,
    m_stage,
    v_all,
    v_stage,
    s_all,
    g_stage,
    onehot,
    gains,
    gains_hl,
    own_t,
    term,
    norm,
    recv,
    chi_acc,
    chi_plane,
    chi_xy,
    chi_z,
    fin,
    in_sem,
    ex_send,
    ex_recv,
    rs_send,
    rs_recv,
    ag_send,
    ag_recv,
    fin_send,
    fin_recv,
    xy_send,
    xy_recv,
    z_send,
    z_recv,
):
    nb = vis_in.shape[2]
    total_b = 2 * nb
    half = goff_in.shape[3]
    quarter = half // 2
    side = chips * half
    size = half + quarter
    nx, ny = plane(chips)
    offsets = far_first(chips)
    peers = len(offsets)
    me = lax.axis_index("bl")
    z = lax.axis_index("ch")
    chip = me // 2
    core = me % 2
    sib = chip * 2 + (1 - core)
    px = chip // ny
    py = chip % ny
    lanes = 128

    def there(bl, ch=None):
        return {"bl": bl, "ch": z if ch is None else ch}

    def peer(k):
        return ((px + offsets[k][0]) % nx) * ny + (py + offsets[k][1]) % ny

    def send(src, dst, ssem, rsem, where):
        return pltpu.make_async_remote_copy(
            src_ref=src, dst_ref=dst, send_sem=ssem, recv_sem=rsem,
            device_id=where, device_id_type=pl.DeviceIdType.MESH)

    def along_z(k):
        return there(chip * 2 + (core + k) % 2, (z + k // 2) % nch)

    z_order = sorted(range(1, 2 * nch), key=lambda k: -min(k // 2, nch - k // 2))

    barrier = pltpu.get_barrier_semaphore()
    for k in z_order:
        pl.semaphore_signal(barrier, inc=1, device_id=along_z(k),
                            device_id_type=pl.DeviceIdType.MESH)
    for k in range(peers):
        pl.semaphore_signal(barrier, inc=1, device_id=there(peer(k) * 2 + core),
                            device_id_type=pl.DeviceIdType.MESH)

    loads = [
        pltpu.make_async_copy(goff_hbm, goff_in, in_sem.at[0]),
        pltpu.make_async_copy(model_hbm, model_in, in_sem.at[1]),
        pltpu.make_async_copy(vis_hbm, vis_in, in_sem.at[2]),
        pltpu.make_async_copy(first_hbm, first_in, in_sem.at[3]),
        pltpu.make_async_copy(second_hbm, second_in, in_sem.at[4]),
    ]
    for load in loads:
        load.start()

    r = lax.broadcasted_iota(jnp.int32, (256, 256), 0)
    q = lax.broadcasted_iota(jnp.int32, (256, 256), 1)
    chan = 2 * ((core + r // 128) & 1) + (r // 64) % 2
    perm = jnp.where(q == (r % 8) * 32 + ((r // 8) % 8) * 4 + chan, 1.0, 0.0).astype(BF16)

    loads[0].wait()
    offs = goff_in[...].reshape(256, half)
    hi = offs.astype(BF16)
    rest = offs - hi.astype(F32)
    mid = rest.astype(BF16)
    low = (rest - mid.astype(F32)).astype(BF16)
    turned = [jnp.dot(perm, one, preferred_element_type=F32) for one in (hi, mid, low)]
    comp = (lax.broadcasted_iota(jnp.int32, (256, half), 0) // 8) % 8
    start = jnp.where((comp == 0) | (comp == 6), 1.0, 0.0) + ((turned[0] + turned[1]) + turned[2])
    here_rows = pl.ds(pl.multiple_of(core * 64, 64), 64)
    for c in range(2):
        own_t[c, here_rows, :] = start[c * 64:c * 64 + 64]
        g_stage[c] = start[128 + c * 64:192 + c * 64]

    loads[1].wait()
    permuted = jnp.dot(perm, model_in[...].reshape(256, nb), preferred_element_type=F32)
    m_all[:, :nb] = permuted[:128]
    m_stage[...] = permuted[128:]
    loads[2].wait()
    for c in range(2):
        for k in range(8):
            row = c * 8 + k
            v_all[row:row + 1, :nb] = vis_in[k, pl.ds(2 * core + c, 1), :]
            v_stage[row:row + 1, :] = vis_in[k, pl.ds(2 * (1 - core) + c, 1), :]
    loads[3].wait()
    loads[4].wait()

    def place(s):
        rem = s % (2 * half)
        return (rem // half) * side + (s // (2 * half)) * half + rem % half

    s_all[0, 0:1, :] = place(first_in[...])
    s_all[0, 1:2, :] = place(second_in[...])
    s_all[0, 2:8, :] = jnp.zeros((6, nb), jnp.int32)

    station = lax.broadcasted_iota(jnp.int32, (STATION_COUNT, BLOCK), 0)

    def hot(part):
        def body(i, carry):
            at = pl.multiple_of(i * BLOCK, BLOCK)
            for j in range(2):
                which = s_all[part, j:j + 1, pl.ds(at, BLOCK)]
                to = pl.multiple_of(j * total_b + part * nb + at, BLOCK)
                onehot[:, pl.ds(to, BLOCK)] = jnp.where(station == which, 1.0, 0.0).astype(BF16)
            return carry

        lax.fori_loop(0, nb // BLOCK, body, 0)

    chi_acc[...] = jnp.zeros_like(chi_acc)
    pl.semaphore_wait(barrier, 2 * nch - 1 + peers)

    swaps = [
        send(g_stage, own_t.at[:, here_rows, :], ex_send.at[0], ex_recv.at[0], there(sib)),
        send(s_all.at[0], s_all.at[1], ex_send.at[1], ex_recv.at[1], there(sib)),
        send(m_stage, m_all.at[:, pl.ds(nb, nb)], ex_send.at[2], ex_recv.at[2], there(sib)),
        send(v_stage, v_all.at[:, pl.ds(nb, nb)], ex_send.at[3], ex_recv.at[3], there(sib)),
    ]
    for swap in swaps:
        swap.start()
    chip_rows = pl.ds(pl.multiple_of(chip * half, half), half)

    def ag_copy(c, k):
        return send(gains.at[c, chip_rows, :], gains.at[c, chip_rows, :],
                    ag_send.at[c, k], ag_recv.at[c, k], there(peer(k) * 2 + core))

    swaps[0].wait_recv()
    for c in range(2):
        gains[c, chip_rows, :] = jnp.transpose(own_t[c])
        for k in range(peers):
            ag_copy(c, k).start()
    hot(0)
    swaps[1].wait_recv()
    hot(1)
    swaps[2].wait_recv()
    swaps[3].wait_recv()
    for swap in swaps:
        swap.wait_send()

    def store_pair(c, row, cols, one, two):
        both = jnp.concatenate([one, two], axis=0)
        hi = both.astype(BF16)
        term[c, row:row + 16, cols] = hi
        term[c, 128 + row:144 + row, cols] = (both - hi.astype(F32)).astype(BF16)

    def terms(c, step):
        both = gains_hl[c]
        chi = jnp.zeros((1, lanes), F32)
        for i in range(total_b // BLOCK):
            cols = pl.ds(i * BLOCK, BLOCK)
            cols_q = pl.ds(total_b + i * BLOCK, BLOCK)
            gp = jnp.dot(both, onehot[:, cols], preferred_element_type=F32)
            gp = gp[:64] + gp[64:]
            gq = jnp.dot(both, onehot[:, cols_q], preferred_element_type=F32)
            gq = gq[:64] + gq[64:]

            def part(x):
                return pairs([x[8 * k:8 * k + 8] for k in range(8)])

            jp = part(gp)
            jq = part(gq)
            mod = pairs([m_all[c * 64 + 8 * k:c * 64 + 8 * k + 8, cols] for k in range(8)])
            y_one = matmul22(mod, herm(jq))
            pred = flat(matmul22(jp, y_one))
            y_two = matmul22(herm(mod), herm(jp))
            resid = []
            for k in range(8):
                one = v_all[c * 8 + k:c * 8 + k + 1, cols] - jnp.sum(pred[k], axis=0, keepdims=True)
                for j in range(0, BLOCK, lanes):
                    chi = chi + one[:, j:j + lanes] * one[:, j:j + lanes]
                resid.append(one)
            resid = pairs(resid)
            a_one = flat(matmul22(resid, herm(y_one))) + gram_parts(y_one)
            a_two = flat(matmul22(herm(resid), herm(y_two))) + gram_parts(y_two)
            for k in range(0, 12, 2):
                store_pair(c, 8 * k, cols, a_one[k], a_one[k + 1])
                store_pair(c, 8 * k, cols_q, a_two[k], a_two[k + 1])
        chi_acc[pl.ds(step, 1), :] += chi

    lane_a = lax.broadcasted_iota(jnp.int32, (side, lanes), 1)
    lane_b = lax.broadcasted_iota(jnp.int32, (quarter, lanes), 1)

    def rs_copy(c, k):
        return send(norm.at[c, peer(k)], recv.at[c, k], rs_send.at[c, k], rs_recv.at[c, k],
                    there(peer(k) * 2 + core))

    def scatter(c):
        sums = nt_dot(onehot[...], term[c])
        sums = sums[:, :lanes] + sums[:, lanes:]
        lower = sums[:side]
        upper = pltpu.roll(sums[side:], 64, 1)
        packed = jnp.where(lane_a < 64, lower, upper)
        for j in range(chips):
            norm[c, j, :half, :] = packed[j * half:(j + 1) * half]
            mid_row = j * half + quarter
            end = (j + 1) * half
            low_one = lower[j * half:mid_row]
            low_two = pltpu.roll(lower[mid_row:end], 32, 1)
            up_one = upper[j * half:mid_row]
            up_two = pltpu.roll(upper[mid_row:end], 32, 1)
            norm[c, j, half:size, :] = jnp.where(
                lane_b < 64,
                jnp.where(lane_b < 32, up_one, up_two),
                jnp.where(lane_b < 96, low_one, low_two))
        for k in range(peers):
            rs_copy(c, k).start()

    def solve(c):
        total = norm[c, chip]
        for k in reversed(range(peers)):
            rs_copy(c, k).wait_recv()
            total = total + recv[c, k]
        r_t = jnp.transpose(total[:half])
        b_t = jnp.transpose(jnp.concatenate(
            [total[half:], pltpu.roll(total[half:], 96, 1)], axis=0))
        fresh_rows = []
        for h in range(2):
            old = [own_t[c, h * 64 + 8 * k:h * 64 + 8 * k + 8, :] for k in range(8)]
            amat = pairs([r_t[h * 64 + 8 * k:h * 64 + 8 * k + 8, :] - old[k] for k in range(8)])
            base = 64 * (1 - h)
            diag_one, diag_two, off_re, off_im = [
                b_t[base + 8 * k:base + 8 * k + 8, :] for k in range(4)]
            diag_one = diag_one + REG
            diag_two = diag_two + REG
            det = diag_one * diag_two - off_re * off_re - off_im * off_im
            scale = 0.5 / det
            d_one = diag_one * scale
            d_two = diag_two * scale
            o_re = off_re * scale
            o_im = off_im * scale
            for row in range(2):
                a0 = amat[2 * row]
                a1 = amat[2 * row + 1]
                n0 = cadd((a0[0] * d_two, a0[1] * d_two), cmul(a1, (-o_re, o_im)))
                n1 = cadd(cmul(a0, (-o_re, -o_im)), (a1[0] * d_one, a1[1] * d_one))
                k = 4 * row
                fresh_rows += [old[k] + n0[0], old[k + 1] + n0[1],
                               old[k + 2] + n1[0], old[k + 3] + n1[1]]
        fresh = jnp.concatenate(fresh_rows, axis=0)
        own_t[c] = fresh
        return jnp.transpose(fresh)

    def prepare(c):
        for k in reversed(range(peers)):
            ag_copy(c, k).wait_recv()
        turned = jnp.transpose(gains[c])
        turned = jnp.concatenate([turned[:64], turned[64:]], axis=1)
        hi = turned.astype(BF16)
        gains_hl[c, :64] = hi
        gains_hl[c, 64:] = (turned - hi.astype(F32)).astype(BF16)

    def after_scatter(c):
        for k in range(peers):
            ag_copy(c, k).wait_send()

    def after_solve(c):
        for k in range(peers):
            rs_copy(c, k).wait_send()

    def early(step, carry):
        for c in range(2):
            prepare(c)
            terms(c, step)
            scatter(c)
            after_scatter(c)
        for c in range(2):
            gains[c, chip_rows, :] = solve(c)
            for k in range(peers):
                ag_copy(c, k).start()
            after_solve(c)
        return carry

    lax.fori_loop(0, ITERS - 1, early, 0)

    def xy_copy(k):
        return send(chi_acc, chi_xy.at[k], xy_send.at[k], xy_recv.at[k],
                    there(peer(k) * 2 + core))

    def z_copy(k):
        return send(chi_plane, chi_z.at[k - 1], z_send.at[k - 1], z_recv.at[k - 1], along_z(k))

    def up(c, which):
        return send(fin.at[1, core, c], fin.at[0, core, c], fin_send.at[c, which],
                    fin_recv.at[0, core, c], there(chip * 2 + which, (z + 1) % nch))

    def down(c, which):
        return send(fin.at[1, core, c], fin.at[2, core, c], fin_send.at[c, 2 + which],
                    fin_recv.at[2, core, c], there(chip * 2 + which, (z + nch - 1) % nch))

    def across(c):
        return send(fin.at[1, core, c], fin.at[1, core, c], fin_send.at[c, 4],
                    fin_recv.at[1, core, c], there(sib))

    def halo(c):
        fin[1, core, c] = solve(c)

        @pl.when(z < nch - 1)
        def _():
            for which in range(2):
                up(c, which).start()

        @pl.when(z > 0)
        def _():
            for which in range(2):
                down(c, which).start()

        across(c).start()

    for c in range(2):
        prepare(c)
        terms(c, ITERS - 1)
        if c == 1:
            for k in range(peers):
                xy_copy(k).start()
        scatter(c)
        after_scatter(c)

    @pl.when(z == 0)
    def _():
        fin[0] = jnp.zeros(fin.shape[1:], F32)

    @pl.when(z == nch - 1)
    def _():
        fin[2] = jnp.zeros(fin.shape[1:], F32)

    shape = (12 * half, 4 * lanes)
    row = lax.broadcasted_iota(jnp.int32, shape, 0)
    col = lax.broadcasted_iota(jnp.int32, shape, 1)
    to = col // lanes
    shift = row // half - 4 - to

    def weigh(step):
        step = step.astype(F32)
        return jnp.exp(-(step * step) / (2.0 * KERNEL_VAR))

    line = lax.broadcasted_iota(jnp.int32, (1, 4 * lanes), 1) // lanes
    denom = jnp.zeros((1, 4 * lanes), F32)
    for s in range(-SPAN, SPAN + 1):
        at = z * 4 + line + s
        denom = denom + jnp.where((at >= 0) & (at < 4 * nch), weigh(jnp.full((1, 4 * lanes), s, jnp.int32)), 0.0)
    mixing = jnp.where(
        (row % half == col % lanes) & (shift >= -SPAN) & (shift <= SPAN), weigh(shift) / denom, 0.0)

    halo(0)
    chi = chi_acc[...]
    for k in reversed(range(peers)):
        xy_copy(k).wait_recv()
        chi = chi + chi_xy[k]
    chi_plane[...] = chi
    for k in z_order:
        z_copy(k).start()
    halo(1)
    for c in range(2):
        after_solve(c)

    def wait_fin(slot, source):
        for c in range(2):
            send(fin.at[slot, source, c], fin.at[slot, source, c], fin_send.at[c, 0],
                 fin_recv.at[slot, source, c], there(sib)).wait_recv()

    wait_fin(1, 1 - core)

    @pl.when(z > 0)
    def _():
        for source in range(2):
            wait_fin(0, source)

    @pl.when(z < nch - 1)
    def _():
        for source in range(2):
            wait_fin(2, source)

    slabs = jnp.transpose(fin[...].reshape(12 * half, lanes))
    slabs = jnp.where(core == 0, slabs[:64], slabs[64:])
    smooth = jnp.dot(slabs, mixing, precision=lax.Precision.HIGHEST, preferred_element_type=F32)
    for c in range(4):
        out_ref[c] = smooth[:, c * lanes:c * lanes + half]

    chi = chi_plane[...]
    for k in reversed(z_order):
        z_copy(k).wait_recv()
        chi = chi + chi_z[k - 1]
    chi_ref[...] = jnp.broadcast_to(jnp.sum(chi, axis=1, keepdims=True), (8, lanes))

    for k in range(peers):
        xy_copy(k).wait_send()
    for k in z_order:
        z_copy(k).wait_send()
    for c in range(2):
        across(c).wait_send()

    @pl.when(z < nch - 1)
    def _():
        for c in range(2):
            for which in range(2):
                up(c, which).wait_send()

    @pl.when(z > 0)
    def _():
        for c in range(2):
            for which in range(2):
                down(c, which).wait_send()


def on_device(visibilities, model, first_station, second_station, gain_offset):
    nb = visibilities.shape[2]
    half = gain_offset.shape[3]
    chips = lax.axis_size("bl") // 2
    nch = lax.axis_size("ch")
    size = half + half // 2
    total_b = 2 * nb
    peers = chips - 1
    vmem = pl.BlockSpec(memory_space=pltpu.VMEM)
    hbm = pl.BlockSpec(memory_space=pltpu.HBM)
    dma = pltpu.SemaphoreType.DMA
    smooth, chi = pl.pallas_call(
        functools.partial(kernel, chips, nch),
        out_shape=(
            jax.ShapeDtypeStruct((4, 64, half), F32),
            jax.ShapeDtypeStruct((8, 128), F32),
        ),
        in_specs=[hbm] * 5,
        out_specs=(vmem, vmem),
        scratch_shapes=[
            pltpu.VMEM(visibilities.shape, F32),
            pltpu.VMEM(model.shape, BF16),
            pltpu.VMEM((1, nb), jnp.int32),
            pltpu.VMEM((1, nb), jnp.int32),
            pltpu.VMEM(gain_offset.shape, F32),
            pltpu.VMEM((128, total_b), F32),
            pltpu.VMEM((128, nb), F32),
            pltpu.VMEM((16, total_b), F32),
            pltpu.VMEM((16, nb), F32),
            pltpu.VMEM((2, 8, nb), jnp.int32),
            pltpu.VMEM((2, 64, half), F32),
            pltpu.VMEM((STATION_COUNT, 2 * total_b), BF16),
            pltpu.VMEM((2, chips * half, 128), F32),
            pltpu.VMEM((2, 128, STATION_COUNT), BF16),
            pltpu.VMEM((2, 128, half), F32),
            pltpu.VMEM((2, 256, 2 * total_b), BF16),
            pltpu.VMEM((2, chips, size, 128), F32),
            pltpu.VMEM((2, peers, size, 128), F32),
            pltpu.VMEM((8, 128), F32),
            pltpu.VMEM((8, 128), F32),
            pltpu.VMEM((peers, 8, 128), F32),
            pltpu.VMEM((2 * nch - 1, 8, 128), F32),
            pltpu.VMEM((3, 2, 2, half, 128), F32),
            dma((5,)),
            dma((4,)),
            dma((4,)),
            dma((2, peers)),
            dma((2, peers)),
            dma((2, peers)),
            dma((2, peers)),
            dma((2, 5)),
            dma((3, 2, 2)),
            dma((peers,)),
            dma((peers,)),
            dma((2 * nch - 1,)),
            dma((2 * nch - 1,)),
        ],
        compiler_params=pltpu.CompilerParams(
            collective_id=0, has_side_effects=True, vmem_limit_bytes=48 * 1024 * 1024),
    )(visibilities, model, first_station[None], second_station[None], gain_offset)
    smoothed = jnp.transpose(smooth.reshape(4, 8, 8, half), (2, 1, 0, 3))
    count_vis = 8.0 * nb * lax.axis_size("bl") * 4 * nch
    misfit = chi[:ITERS, 0] / count_vis
    return (smoothed, misfit)


def solution(mesh):
    return jax.shard_map(
        on_device,
        mesh=mesh,
        in_specs=(
            P(None, "ch", "bl"),
            P(None, None, "ch", "bl"),
            P("bl"),
            P("bl"),
            P(None, None, "ch", "bl"),
        ),
        out_specs=(P(None, None, "ch", "bl"), P()),
        check_vma=False,
    )
```

time: 1090 us -> 63.2 us (0.06)
  other arithmetic: 457 us -> 0.63 us
  waiting for transfers between devices: 259 us -> 0 us
  local copies, waits for them, and re-layouts: 232 us -> 4.79 us
  blocking collectives: 114 us -> 0 us
  Pallas kernels: 0 us -> 56.9 us
  between operations: 15.1 us -> 0.65 us
    scatter-add x6 -> x0, other arithmetic: 405 us -> none  [the longest x3 202 us: accumulate(): jax.ops.segment_sum(jnp.moveaxis(term_q, 3, 0), second_station, num_segme...]
    psum x3 -> x0, waiting for transfers between devices: 257 us -> none  [on_device(): normals = lax.psum(partial_value, 'bl')]
    gather x12 -> x0, local copies, waits for them, and re-layouts: 81.5 us -> none  [the longest x6 41 us: on_device(): gain_p = jnp.take(full, first_station, axis=3)]
    psum x1 -> x0, blocking collectives: 77.7 us -> none  [on_device(): chis.append(lax.psum(chi, ('bl', 'ch')))]
    pallas_call x0 -> x1, Pallas kernels: none -> 56.9 us  [on_device(): pl.pallas_call(functools.partial(kernel, chips, nch), out_shape=(jax.Shap...]
    transpose x6 -> x0, local copies, waits for them, and re-layouts: 50.6 us -> none  [the longest x3 25.6 us: accumulate(): jnp.moveaxis(term_q, 3, 0)]
    all_gather x1 -> x0, blocking collectives: 36.7 us -> none  [on_device(): full = lax.all_gather(own_gains, 'bl', axis=3, tiled=True)]
    scatter-add x6 -> x0, local copies, waits for them, and re-layouts: 34.1 us -> none  [the longest x3 17.4 us: accumulate(): jax.ops.segment_sum(jnp.moveaxis(term_q, 3, 0), second_station, num_segme...]
  transfers between devices with their start and end apart: 5 -> 0, of which waited for: 4 -> 0; matrix products, arithmetic and copies ran while one was open for 1% -> 0% of each run, Pallas kernels for 0% -> 0%
where the time goes in v2:
time: 63.2 us; the launch traced here: 62.9 us
  Pallas kernels  56.9 us (90%)
  local copies, waits for them, and re-layouts  4.79 us (8%)
  between operations  0.65 us (1%)
    pallas_call x1, Pallas kernels, on_device(): pl.pallas_call(functools.partial(kernel, chips, nch), out_shape=(jax.Shap...  56.9 us
    unnamed x10, local copies, waits for them, and re-layouts  4.05 us

profile of v2, /device:TPU:1, one launch (start us, length us, event | category | flops | bytes accessed | tf_op | source)
XLA Modules:
  0.0 62.9 jit_solution(13573207830733878283)
XLA Ops:
  0.6 0.0 copy-start.3
  0.6 0.7 %copy-done.3 = s32[512]{0:T(512)S(1)} copy-done((s32[512]{0:T(512)S(1)}, s32[512]{0:T(512)}, u32[]{:S(2)}) %copy-start.3) | copy-done | bytes 2072
  1.3 0.0 copy-start
  1.3 0.9 %copy-done = bf16[8,8,4,512]{3,2,1,0:T(4,128)(2,1)S(1)} copy-done((bf16[8,8,4,512]{3,2,1,0:T(4,128)(2,1)S(1)}, bf16[8,8,4,512]{3,2,1,0:T(4,128)(2,1)}, u32[]{:S(2)}) %copy-start) | copy-done | bytes 262168
  2.3 0.0 copy-start.1
  2.3 0.9 %copy-done.1 = f32[8,8,4,16]{3,2,1,0:T(4,128)S(1)} copy-done((f32[8,8,4,16]{3,2,1,0:T(4,128)S(1)}, f32[8,8,4,16]{3,2,1,0:T(4,128)}, u32[]{:S(2)}) %copy-start.1) | copy-done | bytes 16408
  3.2 0.0 copy-start.2
  3.2 0.8 %copy-done.2 = f32[8,4,512]{2,1,0:T(4,128)S(1)} copy-done((f32[8,4,512]{2,1,0:T(4,128)S(1)}, f32[8,4,512]{2,1,0:T(4,128)}, u32[]{:S(2)}) %copy-start.2) | copy-done | bytes 65560
  4.0 0.0 copy-start.4
  4.0 0.7 %copy-done.4 = s32[512]{0:T(512)S(1)} copy-done((s32[512]{0:T(512)S(1)}, s32[512]{0:T(512)}, u32[]{:S(2)}) %copy-start.4) | copy-done | bytes 2072
  4.7 56.9 %shard_map.68 = (f32[4,64,16]{2,1,0:T(8,128)S(1)}, f32[8,128]{1,0:T(8,128)S(1)}) custom-call(f32[8,4,512]{2,1,0:T(4,128)S(1)} %copy-done.2, bf16[8,8,4,512]{3,2,1,0:T(4,128)(2,1)S(1)} %copy-done, s32[1,512]{1,0:T(1,128)S(1)} %bitcast.7, s32[1,512]{1,0:T(1,128)S(1)} %bitcast.8, f32[8,8,4,16]{3,2,1,0:T(4,128)S(1)} %copy-done.1), custom_call_target="tpu_custom_call" | custom-call | tf_op jit(solution)/shard_map/pallas_call | solution.py:539
  61.6 0.7 %copy.10 = f32[4,8,8,16]{3,0,1,2:T(4,128)} copy(f32[4,8,8,16]{3,2,1,0:T(8,128)S(1)} %bitcast.6) | data formatting | bytes 32768 | tf_op jit(solution)/shard_map/reshape | solution.py:588
  62.3 0.6 multiply_reduce_fusion
Async XLA Ops:
  0.6 0.7 %copy-start.3 = (s32[512]{0:T(512)S(1)}, s32[512]{0:T(512)}, u32[]{:S(2)}) copy-start(s32[512]{0:T(512)} %param.7) | copy-start | bytes 6148
  1.3 0.9 %copy-start = (bf16[8,8,4,512]{3,2,1,0:T(4,128)(2,1)S(1)}, bf16[8,8,4,512]{3,2,1,0:T(4,128)(2,1)}, u32[]{:S(2)}) copy-start(bf16[8,8,4,512]{3,2,1,0:T(4,128)(2,1)} %model_hbm.1) | copy-start | bytes 786436
  2.3 0.9 %copy-start.1 = (f32[8,8,4,16]{3,2,1,0:T(4,128)S(1)}, f32[8,8,4,16]{3,2,1,0:T(4,128)}, u32[]{:S(2)}) copy-start(f32[8,8,4,16]{3,2,1,0:T(4,128)} %goff_hbm.1) | copy-start | bytes 49156
  3.2 0.8 %copy-start.2 = (f32[8,4,512]{2,1,0:T(4,128)S(1)}, f32[8,4,512]{2,1,0:T(4,128)}, u32[]{:S(2)}) copy-start(f32[8,4,512]{2,1,0:T(4,128)} %vis_hbm.1) | copy-start | bytes 196612
  4.0 0.7 %copy-start.4 = (s32[512]{0:T(512)S(1)}, s32[512]{0:T(512)}, u32[]{:S(2)}) copy-start(s32[512]{0:T(512)} %param.8) | copy-start | bytes 6148

commit v3 on v2

--- a/solution.py
+++ b/solution.py
@@ -584,7 +584,7 @@
         ],
         compiler_params=pltpu.CompilerParams(
             collective_id=0, has_side_effects=True, vmem_limit_bytes=48 * 1024 * 1024),
-    )(visibilities, model, first_station[None], second_station[None], gain_offset)
+    )(*[pltpu.with_memory_space_constraint(x, pltpu.HBM) for x in (visibilities, model, first_station[None], second_station[None], gain_offset)])
     smoothed = jnp.transpose(smooth.reshape(4, 8, 8, half), (2, 1, 0, 3))
     count_vis = 8.0 * nb * lax.axis_size("bl") * 4 * nch
     misfit = chi[:ITERS, 0] / count_vis

time: 63.2 us -> 59.1 us (0.935)
  local copies, waits for them, and re-layouts: 4.79 us -> 0.74 us
    unnamed x10 -> x0, local copies, waits for them, and re-layouts: 4.05 us -> none
where the time goes in v3:
time: 59.1 us; the launch traced here: 59 us
  Pallas kernels  57 us (96%)
  local copies, waits for them, and re-layouts  0.74 us (1%)
  between operations  0.64 us (1%)
  other arithmetic  0.63 us (1%)
    pallas_call x1, Pallas kernels, on_device(): pl.pallas_call(functools.partial(kernel, chips, nch), out_shape=(jax.Shap...  57 us

profile of v3, /device:TPU:1, one launch (start us, length us, event | category | flops | bytes accessed | tf_op | source)
XLA Modules:
  0.0 59.0 jit_solution(4539625256107868906)
XLA Ops:
  0.6 57.0 %shard_map.68 = (f32[4,64,16]{2,1,0:T(8,128)S(1)}, f32[8,128]{1,0:T(8,128)S(1)}) custom-call(f32[8,4,512]{2,1,0:T(4,128)} %vis_hbm.1, bf16[8,8,4,512]{3,2,1,0:T(4,128)(2,1)} %model_hbm.1, s32[1,512]{1,0:T(1,128)} %bitcast.8, s32[1,512]{1,0:T(1,128)} %bitcast.9, f32[8,8,4,16]{3,2,1,0:T(4,128)} %goff_hbm.1), custom_call_target="tpu_custom_call" | custom-call | tf_op jit(solution)/shard_map/pallas_call | solution.py:539
  57.7 0.7 %copy.10 = f32[4,8,8,16]{3,0,1,2:T(4,128)} copy(f32[4,8,8,16]{3,2,1,0:T(8,128)S(1)} %bitcast.6) | data formatting | bytes 32768 | tf_op jit(solution)/shard_map/reshape | solution.py:588
  58.4 0.6 %multiply_reduce_fusion = f32[3]{0:T(128)} fusion(f32[8,128]{1,0:T(8,128)S(1)} %get-tuple-element.5), kind=kLoop, calls=%fused_computation.1 | loop fusion | flops 3 | bytes 24 | tf_op jit(solution)/shard_map/div | solution.py:590

commit v4 on v3

--- a/solution.py
+++ b/solution.py
@@ -13,6 +13,7 @@
 REG = 1.0
 KERNEL_VAR = 4.0
 BLOCK = 256
+HELD = 3
 F32 = jnp.float32
 BF16 = jnp.bfloat16
 
@@ -177,9 +178,15 @@
     for load in loads:
         load.start()
 
+    def mine(c, work):
+        if c == 0:
+            work()
+        else:
+            pl.when(core == 1)(work)
+
     r = lax.broadcasted_iota(jnp.int32, (256, 256), 0)
     q = lax.broadcasted_iota(jnp.int32, (256, 256), 1)
-    chan = 2 * ((core + r // 128) & 1) + (r // 64) % 2
+    chan = (r // 64 + core) % 4
     perm = jnp.where(q == (r % 8) * 32 + ((r // 8) % 8) * 4 + chan, 1.0, 0.0).astype(BF16)
 
     loads[0].wait()
@@ -192,20 +199,36 @@
     comp = (lax.broadcasted_iota(jnp.int32, (256, half), 0) // 8) % 8
     start = jnp.where((comp == 0) | (comp == 6), 1.0, 0.0) + ((turned[0] + turned[1]) + turned[2])
     here_rows = pl.ds(pl.multiple_of(core * 64, 64), 64)
-    for c in range(2):
+    for c in range(HELD):
         own_t[c, here_rows, :] = start[c * 64:c * 64 + 64]
-        g_stage[c] = start[128 + c * 64:192 + c * 64]
+
+    @pl.when(core == 0)
+    def _():
+        for c in range(HELD):
+            g_stage[c] = start[(c + 1) * 64:(c + 2) * 64]
+
+    @pl.when(core == 1)
+    def _():
+        g_stage[0] = start[192:]
 
     loads[1].wait()
     permuted = jnp.dot(perm, model_in[...].reshape(256, nb), preferred_element_type=F32)
-    m_all[:, :nb] = permuted[:128]
-    m_stage[...] = permuted[128:]
+    m_all[:, :nb] = permuted[:192]
+
+    @pl.when(core == 0)
+    def _():
+        m_stage[...] = permuted[64:]
+
+    @pl.when(core == 1)
+    def _():
+        m_stage[:64] = permuted[192:]
+
     loads[2].wait()
-    for c in range(2):
+    for c in range(HELD):
         for k in range(8):
             row = c * 8 + k
-            v_all[row:row + 1, :nb] = vis_in[k, pl.ds(2 * core + c, 1), :]
-            v_stage[row:row + 1, :] = vis_in[k, pl.ds(2 * (1 - core) + c, 1), :]
+            v_all[row:row + 1, :nb] = vis_in[k, pl.ds(core + c, 1), :]
+            v_stage[row:row + 1, :] = vis_in[k, pl.ds(1 - core + c, 1), :]
     loads[3].wait()
     loads[4].wait()
 
@@ -217,46 +240,60 @@
     s_all[0, 1:2, :] = place(second_in[...])
     s_all[0, 2:8, :] = jnp.zeros((6, nb), jnp.int32)
 
-    station = lax.broadcasted_iota(jnp.int32, (STATION_COUNT, BLOCK), 0)
-
     def hot(part):
-        def body(i, carry):
-            at = pl.multiple_of(i * BLOCK, BLOCK)
+        for i in range(nb // BLOCK):
             for j in range(2):
-                which = s_all[part, j:j + 1, pl.ds(at, BLOCK)]
-                to = pl.multiple_of(j * total_b + part * nb + at, BLOCK)
-                onehot[:, pl.ds(to, BLOCK)] = jnp.where(station == which, 1.0, 0.0).astype(BF16)
-            return carry
-
-        lax.fori_loop(0, nb // BLOCK, body, 0)
+                which = s_all[part, j:j + 1, i * BLOCK:(i + 1) * BLOCK]
+                to = j * total_b + part * nb + i * BLOCK
+                station = lax.broadcasted_iota(jnp.int32, (STATION_COUNT, BLOCK), 0)
+                onehot[:, to:to + BLOCK] = jnp.where(station == which, 1.0, 0.0).astype(BF16)
 
     chi_acc[...] = jnp.zeros_like(chi_acc)
     pl.semaphore_wait(barrier, 2 * nch - 1 + peers)
 
+    def swap_pair(count):
+        return [
+            send(g_stage.at[pl.ds(0, count)], own_t.at[pl.ds(0, count), here_rows, :],
+                 ex_send.at[0], ex_recv.at[0], there(sib)),
+            send(m_stage.at[pl.ds(0, count * 64)], m_all.at[pl.ds(0, count * 64), pl.ds(nb, nb)],
+                 ex_send.at[2], ex_recv.at[2], there(sib)),
+        ]
+
+    give = {0: swap_pair(HELD), 1: swap_pair(1)}
     swaps = [
-        send(g_stage, own_t.at[:, here_rows, :], ex_send.at[0], ex_recv.at[0], there(sib)),
         send(s_all.at[0], s_all.at[1], ex_send.at[1], ex_recv.at[1], there(sib)),
-        send(m_stage, m_all.at[:, pl.ds(nb, nb)], ex_send.at[2], ex_recv.at[2], there(sib)),
         send(v_stage, v_all.at[:, pl.ds(nb, nb)], ex_send.at[3], ex_recv.at[3], there(sib)),
     ]
+
+    def per_core(what):
+        for which in range(2):
+            @pl.when(core == which)
+            def _():
+                what(which)
+
+    per_core(lambda which: [one.start() for one in give[which]] and None)
     for swap in swaps:
         swap.start()
     chip_rows = pl.ds(pl.multiple_of(chip * half, half), half)
 
     def ag_copy(c, k):
         return send(gains.at[c, chip_rows, :], gains.at[c, chip_rows, :],
-                    ag_send.at[c, k], ag_recv.at[c, k], there(peer(k) * 2 + core))
-
+                    ag_send.at[c], ag_recv.at[c], there(peer(k) * 2 + core))
+
+    per_core(lambda which: give[1 - which][0].wait_recv())
+    for c in range(HELD):
+        def gather_start():
+            gains[c, chip_rows, :] = jnp.transpose(own_t[c])
+            for k in range(peers):
+                ag_copy(c, k).start()
+
+        mine(c, gather_start)
+    hot(0)
     swaps[0].wait_recv()
-    for c in range(2):
-        gains[c, chip_rows, :] = jnp.transpose(own_t[c])
-        for k in range(peers):
-            ag_copy(c, k).start()
-    hot(0)
+    hot(1)
+    per_core(lambda which: give[1 - which][1].wait_recv())
     swaps[1].wait_recv()
-    hot(1)
-    swaps[2].wait_recv()
-    swaps[3].wait_recv()
+    per_core(lambda which: [one.wait_send() for one in give[which]] and None)
     for swap in swaps:
         swap.wait_send()
 
@@ -304,7 +341,7 @@
     lane_b = lax.broadcasted_iota(jnp.int32, (quarter, lanes), 1)
 
     def rs_copy(c, k):
-        return send(norm.at[c, peer(k)], recv.at[c, k], rs_send.at[c, k], rs_recv.at[c, k],
+        return send(norm.at[c, peer(k)], recv.at[c, k], rs_send.at[c], rs_recv.at[c],
                     there(peer(k) * 2 + core))
 
     def scatter(c):
@@ -328,10 +365,17 @@
         for k in range(peers):
             rs_copy(c, k).start()
 
+    def rs_whole(c):
+        return send(norm.at[c, pl.ds(0, peers)], recv.at[c], rs_send.at[c], rs_recv.at[c], there(sib))
+
+    def ag_whole(c):
+        part = gains.at[c, pl.ds(0, peers * half), :]
+        return send(part, part, ag_send.at[c], ag_recv.at[c], there(sib))
+
     def solve(c):
         total = norm[c, chip]
-        for k in reversed(range(peers)):
-            rs_copy(c, k).wait_recv()
+        rs_whole(c).wait_recv()
+        for k in range(peers):
             total = total + recv[c, k]
         r_t = jnp.transpose(total[:half])
         b_t = jnp.transpose(jnp.concatenate(
@@ -364,8 +408,7 @@
         return jnp.transpose(fresh)
 
     def prepare(c):
-        for k in reversed(range(peers)):
-            ag_copy(c, k).wait_recv()
+        ag_whole(c).wait_recv()
         turned = jnp.transpose(gains[c])
         turned = jnp.concatenate([turned[:64], turned[64:]], axis=1)
         hi = turned.astype(BF16)
@@ -373,49 +416,56 @@
         gains_hl[c, 64:] = (turned - hi.astype(F32)).astype(BF16)
 
     def after_scatter(c):
-        for k in range(peers):
-            ag_copy(c, k).wait_send()
+        ag_whole(c).wait_send()
 
     def after_solve(c):
-        for k in range(peers):
-            rs_copy(c, k).wait_send()
+        rs_whole(c).wait_send()
 
     def early(step, carry):
-        for c in range(2):
-            prepare(c)
-            terms(c, step)
-            scatter(c)
-            after_scatter(c)
-        for c in range(2):
-            gains[c, chip_rows, :] = solve(c)
-            for k in range(peers):
-                ag_copy(c, k).start()
-            after_solve(c)
+        for c in range(HELD):
+            def forth():
+                prepare(c)
+                terms(c, step)
+                scatter(c)
+                after_scatter(c)
+
+            mine(c, forth)
+        for c in range(HELD):
+            def back():
+                gains[c, chip_rows, :] = solve(c)
+                for k in range(peers):
+                    ag_copy(c, k).start()
+                after_solve(c)
+
+            mine(c, back)
         return carry
 
     lax.fori_loop(0, ITERS - 1, early, 0)
 
     def xy_copy(k):
-        return send(chi_acc, chi_xy.at[k], xy_send.at[k], xy_recv.at[k],
+        return send(chi_acc, chi_xy.at[k], xy_send.at[0], xy_recv.at[0],
                     there(peer(k) * 2 + core))
 
     def z_copy(k):
-        return send(chi_plane, chi_z.at[k - 1], z_send.at[k - 1], z_recv.at[k - 1], along_z(k))
+        return send(chi_plane, chi_z.at[k - 1], z_send.at[0], z_recv.at[0], along_z(k))
 
     def up(c, which):
-        return send(fin.at[1, core, c], fin.at[0, core, c], fin_send.at[c, which],
-                    fin_recv.at[0, core, c], there(chip * 2 + which, (z + 1) % nch))
+        g = core + c
+        return send(fin.at[1, g], fin.at[0, g], fin_send.at[c, which],
+                    fin_recv.at[0, g], there(chip * 2 + which, (z + 1) % nch))
 
     def down(c, which):
-        return send(fin.at[1, core, c], fin.at[2, core, c], fin_send.at[c, 2 + which],
-                    fin_recv.at[2, core, c], there(chip * 2 + which, (z + nch - 1) % nch))
+        g = core + c
+        return send(fin.at[1, g], fin.at[2, g], fin_send.at[c, 2 + which],
+                    fin_recv.at[2, g], there(chip * 2 + which, (z + nch - 1) % nch))
 
     def across(c):
-        return send(fin.at[1, core, c], fin.at[1, core, c], fin_send.at[c, 4],
-                    fin_recv.at[1, core, c], there(sib))
+        g = core + c
+        return send(fin.at[1, g], fin.at[1, g], fin_send.at[c, 4],
+                    fin_recv.at[1, g], there(sib))
 
     def halo(c):
-        fin[1, core, c] = solve(c)
+        fin[1, core + c] = solve(c)
 
         @pl.when(z < nch - 1)
         def _():
@@ -429,14 +479,22 @@
 
         across(c).start()
 
-    for c in range(2):
-        prepare(c)
-        terms(c, ITERS - 1)
-        if c == 1:
-            for k in range(peers):
-                xy_copy(k).start()
-        scatter(c)
-        after_scatter(c)
+    def xy_start():
+        for k in range(peers):
+            xy_copy(k).start()
+
+    for c in range(HELD):
+        def forth():
+            prepare(c)
+            terms(c, ITERS - 1)
+            if c == 0:
+                pl.when(core == 0)(xy_start)
+            if c == HELD - 1:
+                xy_start()
+            scatter(c)
+            after_scatter(c)
+
+        mine(c, forth)
 
     @pl.when(z == 0)
     def _():
@@ -464,34 +522,44 @@
     mixing = jnp.where(
         (row % half == col % lanes) & (shift >= -SPAN) & (shift <= SPAN), weigh(shift) / denom, 0.0)
 
+    def plane_chi():
+        chi = chi_acc[...]
+        send(chi_xy, chi_xy, xy_send.at[0], xy_recv.at[0], there(sib)).wait_recv()
+        for k in range(peers):
+            chi = chi + chi_xy[k]
+        chi_plane[...] = chi
+        for k in z_order:
+            z_copy(k).start()
+
     halo(0)
-    chi = chi_acc[...]
-    for k in reversed(range(peers)):
-        xy_copy(k).wait_recv()
-        chi = chi + chi_xy[k]
-    chi_plane[...] = chi
-    for k in z_order:
-        z_copy(k).start()
-    halo(1)
-    for c in range(2):
-        after_solve(c)
-
-    def wait_fin(slot, source):
-        for c in range(2):
-            send(fin.at[slot, source, c], fin.at[slot, source, c], fin_send.at[c, 0],
-                 fin_recv.at[slot, source, c], there(sib)).wait_recv()
-
-    wait_fin(1, 1 - core)
+
+    @pl.when(core == 1)
+    def _():
+        halo(1)
+
+    plane_chi()
+
+    @pl.when(core == 1)
+    def _():
+        halo(2)
+
+    for c in range(HELD):
+        mine(c, lambda: after_solve(c))
+
+    def wait_fin(slot, which):
+        for g in which:
+            send(fin.at[slot, g], fin.at[slot, g], fin_send.at[0, 0],
+                 fin_recv.at[slot, g], there(sib)).wait_recv()
+
+    per_core(lambda which: wait_fin(1, range(1, 4) if which == 0 else range(1)))
 
     @pl.when(z > 0)
     def _():
-        for source in range(2):
-            wait_fin(0, source)
+        wait_fin(0, range(4))
 
     @pl.when(z < nch - 1)
     def _():
-        for source in range(2):
-            wait_fin(2, source)
+        wait_fin(2, range(4))
 
     slabs = jnp.transpose(fin[...].reshape(12 * half, lanes))
     slabs = jnp.where(core == 0, slabs[:64], slabs[64:])
@@ -500,29 +568,28 @@
         out_ref[c] = smooth[:, c * lanes:c * lanes + half]
 
     chi = chi_plane[...]
-    for k in reversed(z_order):
-        z_copy(k).wait_recv()
+    send(chi_z, chi_z, z_send.at[0], z_recv.at[0], there(sib)).wait_recv()
+    for k in z_order:
         chi = chi + chi_z[k - 1]
     chi_ref[...] = jnp.broadcast_to(jnp.sum(chi, axis=1, keepdims=True), (8, lanes))
 
-    for k in range(peers):
-        xy_copy(k).wait_send()
-    for k in z_order:
-        z_copy(k).wait_send()
-    for c in range(2):
-        across(c).wait_send()
-
-    @pl.when(z < nch - 1)
-    def _():
-        for c in range(2):
-            for which in range(2):
-                up(c, which).wait_send()
-
-    @pl.when(z > 0)
-    def _():
-        for c in range(2):
-            for which in range(2):
-                down(c, which).wait_send()
+    send(chi_xy, chi_xy, xy_send.at[0], xy_recv.at[0], there(sib)).wait_send()
+    send(chi_z, chi_z, z_send.at[0], z_recv.at[0], there(sib)).wait_send()
+    for c in range(HELD):
+        def finish():
+            across(c).wait_send()
+
+            @pl.when(z < nch - 1)
+            def _():
+                for which in range(2):
+                    up(c, which).wait_send()
+
+            @pl.when(z > 0)
+            def _():
+                for which in range(2):
+                    down(c, which).wait_send()
+
+        mine(c, finish)
 
 
 def on_device(visibilities, model, first_station, second_station, gain_offset):
@@ -550,37 +617,37 @@
             pltpu.VMEM((1, nb), jnp.int32),
             pltpu.VMEM((1, nb), jnp.int32),
             pltpu.VMEM(gain_offset.shape, F32),
-            pltpu.VMEM((128, total_b), F32),
-            pltpu.VMEM((128, nb), F32),
-            pltpu.VMEM((16, total_b), F32),
-            pltpu.VMEM((16, nb), F32),
+            pltpu.VMEM((64 * HELD, total_b), F32),
+            pltpu.VMEM((64 * HELD, nb), F32),
+            pltpu.VMEM((8 * HELD, total_b), F32),
+            pltpu.VMEM((8 * HELD, nb), F32),
             pltpu.VMEM((2, 8, nb), jnp.int32),
-            pltpu.VMEM((2, 64, half), F32),
+            pltpu.VMEM((HELD, 64, half), F32),
             pltpu.VMEM((STATION_COUNT, 2 * total_b), BF16),
-            pltpu.VMEM((2, chips * half, 128), F32),
-            pltpu.VMEM((2, 128, STATION_COUNT), BF16),
-            pltpu.VMEM((2, 128, half), F32),
-            pltpu.VMEM((2, 256, 2 * total_b), BF16),
-            pltpu.VMEM((2, chips, size, 128), F32),
-            pltpu.VMEM((2, peers, size, 128), F32),
+            pltpu.VMEM((HELD, chips * half, 128), F32),
+            pltpu.VMEM((HELD, 128, STATION_COUNT), BF16),
+            pltpu.VMEM((HELD, 128, half), F32),
+            pltpu.VMEM((HELD, 256, 2 * total_b), BF16),
+            pltpu.VMEM((HELD, chips, size, 128), F32),
+            pltpu.VMEM((HELD, peers, size, 128), F32),
             pltpu.VMEM((8, 128), F32),
             pltpu.VMEM((8, 128), F32),
             pltpu.VMEM((peers, 8, 128), F32),
             pltpu.VMEM((2 * nch - 1, 8, 128), F32),
-            pltpu.VMEM((3, 2, 2, half, 128), F32),
+            pltpu.VMEM((3, 4, half, 128), F32),
             dma((5,)),
             dma((4,)),
             dma((4,)),
-            dma((2, peers)),
-            dma((2, peers)),
-            dma((2, peers)),
-            dma((2, peers)),
-            dma((2, 5)),
-            dma((3, 2, 2)),
-            dma((peers,)),
-            dma((peers,)),
-            dma((2 * nch - 1,)),
-            dma((2 * nch - 1,)),
+            dma((HELD,)),
+            dma((HELD,)),
+            dma((HELD,)),
+            dma((HELD,)),
+            dma((HELD, 5)),
+            dma((3, 4)),
+            dma((1,)),
+            dma((1,)),
+            dma((1,)),
+            dma((1,)),
         ],
         compiler_params=pltpu.CompilerParams(
             collective_id=0, has_side_effects=True, vmem_limit_bytes=48 * 1024 * 1024),

time: 59.1 us -> 56.6 us (0.958)
  Pallas kernels: 57 us -> 54.5 us
    pallas_call x1, Pallas kernels: 57 us -> 54.5 us  [on_device(): pl.pallas_call(functools.partial(kernel, chips, nch), out_shape=(jax.Shap...]
where the time goes in v4:
time: 56.6 us; the launch traced here: 56.5 us
  Pallas kernels  54.5 us (96%)
  local copies, waits for them, and re-layouts  0.74 us (1%)
  between operations  0.64 us (1%)
  other arithmetic  0.63 us (1%)
    pallas_call x1, Pallas kernels, on_device(): pl.pallas_call(functools.partial(kernel, chips, nch), out_shape=(jax.Shap...  54.5 us

profile of v4, /device:TPU:1, one launch (start us, length us, event | category | flops | bytes accessed | tf_op | source)
XLA Modules:
  0.0 56.5 jit_solution(566059977568882296)
XLA Ops:
  0.6 54.5 %shard_map.68 = (f32[4,64,16]{2,1,0:T(8,128)S(1)}, f32[8,128]{1,0:T(8,128)S(1)}) custom-call(f32[8,4,512]{2,1,0:T(4,128)} %vis_hbm.1, bf16[8,8,4,512]{3,2,1,0:T(4,128)(2,1)} %model_hbm.1, s32[1,512]{1,0:T(1,128)} %bitcast.8, s32[1,512]{1,0:T(1,128)} %bitcast.9, f32[8,8,4,16]{3,2,1,0:T(4,128)} %goff_hbm.1), custom_call_target="tpu_custom_call" | custom-call | tf_op jit(solution)/shard_map/pallas_call | solution.py:606
  55.1 0.7 %copy.10 = f32[4,8,8,16]{3,0,1,2:T(4,128)} copy(f32[4,8,8,16]{3,2,1,0:T(8,128)S(1)} %bitcast.6) | data formatting | bytes 32768 | tf_op jit(solution)/shard_map/reshape | solution.py:655
  55.9 0.6 %multiply_reduce_fusion = f32[3]{0:T(128)} fusion(f32[8,128]{1,0:T(8,128)S(1)} %get-tuple-element.5), kind=kLoop, calls=%fused_computation.1 | loop fusion | flops 3 | bytes 24 | tf_op jit(solution)/shard_map/div | solution.py:657

commit v5 on v4

--- a/solution.py
+++ b/solution.py
@@ -161,11 +161,11 @@
     z_order = sorted(range(1, 2 * nch), key=lambda k: -min(k // 2, nch - k // 2))
 
     barrier = pltpu.get_barrier_semaphore()
+    for k in range(peers):
+        pl.semaphore_signal(barrier, inc=1, device_id=there(peer(k) * 2 + core),
+                            device_id_type=pl.DeviceIdType.MESH)
     for k in z_order:
         pl.semaphore_signal(barrier, inc=1, device_id=along_z(k),
-                            device_id_type=pl.DeviceIdType.MESH)
-    for k in range(peers):
-        pl.semaphore_signal(barrier, inc=1, device_id=there(peer(k) * 2 + core),
                             device_id_type=pl.DeviceIdType.MESH)
 
     loads = [
@@ -375,8 +375,10 @@
     def solve(c):
         total = norm[c, chip]
         rs_whole(c).wait_recv()
-        for k in range(peers):
-            total = total + recv[c, k]
+        parts = [total] + [recv[c, k] for k in range(peers)]
+        while len(parts) > 1:
+            parts = [sum(parts[j + 1:j + 2], parts[j]) for j in range(0, len(parts), 2)]
+        total = parts[0]
         r_t = jnp.transpose(total[:half])
         b_t = jnp.transpose(jnp.concatenate(
             [total[half:], pltpu.roll(total[half:], 96, 1)], axis=0))
@@ -427,12 +429,13 @@
                 prepare(c)
                 terms(c, step)
                 scatter(c)
-                after_scatter(c)
 
             mine(c, forth)
         for c in range(HELD):
             def back():
-                gains[c, chip_rows, :] = solve(c)
+                rows = solve(c)
+                after_scatter(c)
+                gains[c, chip_rows, :] = rows
                 for k in range(peers):
                     ag_copy(c, k).start()
                 after_solve(c)
@@ -466,6 +469,7 @@
 
     def halo(c):
         fin[1, core + c] = solve(c)
+        after_scatter(c)
 
         @pl.when(z < nch - 1)
         def _():
@@ -492,7 +496,6 @@
             if c == HELD - 1:
                 xy_start()
             scatter(c)
-            after_scatter(c)
 
         mine(c, forth)
 

time: 56.6 us -> 56.3 us (level)
  no operation moved by 1% of the time
where the time goes in v5:
time: 56.3 us; the launch traced here: 56.2 us
  Pallas kernels  54.2 us (96%)
  local copies, waits for them, and re-layouts  0.74 us (1%)
  between operations  0.64 us (1%)
  other arithmetic  0.63 us (1%)
    pallas_call x1, Pallas kernels, on_device(): pl.pallas_call(functools.partial(kernel, chips, nch), out_shape=(jax.Shap...  54.2 us

profile of v5, /device:TPU:1, one launch (start us, length us, event | category | flops | bytes accessed | tf_op | source)
XLA Modules:
  0.0 56.2 jit_solution(1545272677138179451)
XLA Ops:
  0.6 54.2 %shard_map.68 = (f32[4,64,16]{2,1,0:T(8,128)S(1)}, f32[8,128]{1,0:T(8,128)S(1)}) custom-call(f32[8,4,512]{2,1,0:T(4,128)} %vis_hbm.1, bf16[8,8,4,512]{3,2,1,0:T(4,128)(2,1)} %model_hbm.1, s32[1,512]{1,0:T(1,128)} %bitcast.8, s32[1,512]{1,0:T(1,128)} %bitcast.9, f32[8,8,4,16]{3,2,1,0:T(4,128)} %goff_hbm.1), custom_call_target="tpu_custom_call" | custom-call | tf_op jit(solution)/shard_map/pallas_call | solution.py:609
  54.8 0.7 %copy.10 = f32[4,8,8,16]{3,0,1,2:T(4,128)} copy(f32[4,8,8,16]{3,2,1,0:T(8,128)S(1)} %bitcast.6) | data formatting | bytes 32768 | tf_op jit(solution)/shard_map/reshape | solution.py:658
  55.6 0.6 %multiply_reduce_fusion = f32[3]{0:T(128)} fusion(f32[8,128]{1,0:T(8,128)S(1)} %get-tuple-element.5), kind=kLoop, calls=%fused_computation.1 | loop fusion | flops 3 | bytes 24 | tf_op jit(solution)/shard_map/div | solution.py:660

commit v6 on v4

--- a/solution.py
+++ b/solution.py
@@ -306,9 +306,9 @@
     def terms(c, step):
         both = gains_hl[c]
         chi = jnp.zeros((1, lanes), F32)
-        for i in range(total_b // BLOCK):
-            cols = pl.ds(i * BLOCK, BLOCK)
-            cols_q = pl.ds(total_b + i * BLOCK, BLOCK)
+        def body(i, chi):
+            cols = pl.ds(pl.multiple_of(i * BLOCK, BLOCK), BLOCK)
+            cols_q = pl.ds(pl.multiple_of(total_b + i * BLOCK, BLOCK), BLOCK)
             gp = jnp.dot(both, onehot[:, cols], preferred_element_type=F32)
             gp = gp[:64] + gp[64:]
             gq = jnp.dot(both, onehot[:, cols_q], preferred_element_type=F32)
@@ -335,6 +335,9 @@
             for k in range(0, 12, 2):
                 store_pair(c, 8 * k, cols, a_one[k], a_one[k + 1])
                 store_pair(c, 8 * k, cols_q, a_two[k], a_two[k + 1])
+            return chi
+
+        chi = lax.fori_loop(0, total_b // BLOCK, body, chi, unroll=2)
         chi_acc[pl.ds(step, 1), :] += chi
 
     lane_a = lax.broadcasted_iota(jnp.int32, (side, lanes), 1)

time: 56.6 us -> 58.1 us (1.027)
  Pallas kernels: 54.5 us -> 56 us
    pallas_call x1, Pallas kernels: 54.5 us -> 56 us  [on_device(): pl.pallas_call(functools.partial(kernel, chips, nch), out_shape=(jax.Shap...]
where the time goes in v6:
time: 58.1 us; the launch traced here: 58 us
  Pallas kernels  56 us (96%)
  local copies, waits for them, and re-layouts  0.74 us (1%)
  between operations  0.64 us (1%)
  other arithmetic  0.63 us (1%)
    pallas_call x1, Pallas kernels, on_device(): pl.pallas_call(functools.partial(kernel, chips, nch), out_shape=(jax.Shap...  56 us

profile of v6, /device:TPU:1, one launch (start us, length us, event | category | flops | bytes accessed | tf_op | source)
XLA Modules:
  0.0 58.0 jit_solution(13803131140721181007)
XLA Ops:
  0.6 56.0 %shard_map.68 = (f32[4,64,16]{2,1,0:T(8,128)S(1)}, f32[8,128]{1,0:T(8,128)S(1)}) custom-call(f32[8,4,512]{2,1,0:T(4,128)} %vis_hbm.1, bf16[8,8,4,512]{3,2,1,0:T(4,128)(2,1)} %model_hbm.1, s32[1,512]{1,0:T(1,128)} %bitcast.8, s32[1,512]{1,0:T(1,128)} %bitcast.9, f32[8,8,4,16]{3,2,1,0:T(4,128)} %goff_hbm.1), custom_call_target="tpu_custom_call" | custom-call | tf_op jit(solution)/shard_map/pallas_call | solution.py:609
  56.7 0.7 %copy.10 = f32[4,8,8,16]{3,0,1,2:T(4,128)} copy(f32[4,8,8,16]{3,2,1,0:T(8,128)S(1)} %bitcast.6) | data formatting | bytes 32768 | tf_op jit(solution)/shard_map/reshape | solution.py:658
  57.4 0.6 %multiply_reduce_fusion = f32[3]{0:T(128)} fusion(f32[8,128]{1,0:T(8,128)S(1)} %get-tuple-element.5), kind=kLoop, calls=%fused_computation.1 | loop fusion | flops 3 | bytes 24 | tf_op jit(solution)/shard_map/div | solution.py:660
